TPU v7x, 512 devices: a whole 4x4x16 slice. The times are simulated.
512 devices in a mesh: grp: 32 (over z_hi, y, core), vocab: 16 (over z_lo, x).
Axes of the slice: x: 4, y: 4, z: 16 (z_hi: 4, z_lo: 4; z = z_hi * 4 + z_lo), core: 2. Of those that a mesh axis runs over, the one named last changes fastest.
Arguments:
- t_act: bfloat16 [192, 25600], P(None, 'vocab'), may hold values from -6 to 6
- t_down: bfloat16 [25600, 5120], P('vocab', 'grp'), may hold values from -0.0390625 to 0.0390625
- t_resid: bfloat16 [192, 5120], P('vocab', 'grp'), may hold values from -6 to 6
- t_gain: float32 [5120], P('grp'), may hold values from 0.25 to 1.75
- s_hidden: bfloat16 [192, 4096], P('vocab', 'grp'), may hold values from -6 to 6
- t_head: bfloat16 [98304, 5120], P(('grp', 'vocab')), may hold values from -30 to 30
- s_head: bfloat16 [98304, 4096], P(('grp', 'vocab')), may hold values from -30 to 30
- domain_ids: int32 [192], replicated, may hold values from 0 to 7
- domain_counts: int32 [8], replicated, may hold values from 12 to 47
Outputs:
- grad_hidden: float32 [192, 4096], P('vocab', 'grp')
- domain_loss: float32 [8], replicated
All inputs are finite; a program needn't handle non-finite values.
Results may differ from a plain program's by a relative error of at most 0.0067.
Values may be sent and summed in bfloat16 or wider, within the bound.
A program may use at most 64 MiB of HBM per device.

v0:
```python
import jax
import jax.numpy as jnp
from jax import lax
from jax.sharding import PartitionSpec as P

DT = 5120
TOK = 192
NDOM = 8


def logits_of(hidden, head):
    return lax.dot_general(
        hidden, head, (((1,), (1,)), ((), ())), preferred_element_type=jnp.float32
    )


def folding(head, piece):
    return logits_of(piece, head)


def per_device(t_act, t_down, t_resid, t_gain, s_hidden, t_head, s_head, domain_ids, domain_counts):
    partial_sum = jnp.dot(t_act, t_down, preferred_element_type=jnp.float32)
    summed = lax.psum_scatter(partial_sum, "vocab", scatter_dimension=0, tiled=True)
    pre = t_resid.astype(jnp.float32) + summed
    squares = lax.psum(jnp.sum(pre * pre, axis=1, keepdims=True), "grp")
    t_norm = (pre * lax.rsqrt(squares / DT + 1e-06) * t_gain[None, :]).astype(jnp.bfloat16)
    t_rows = lax.all_gather(t_norm, "vocab", axis=0, tiled=True)
    zt = folding(t_head, lax.all_gather(t_rows, "grp", axis=1, tiled=True))
    s_rows = lax.all_gather(s_hidden, "vocab", axis=0, tiled=True)
    zs = folding(s_head, lax.all_gather(s_rows, "grp", axis=1, tiled=True))
    local_t = jnp.max(zt, axis=1)
    local_s = jnp.max(zs, axis=1)
    top_t, top_s = lax.pmax((local_t, local_s), ("grp", "vocab"))
    exp_t = jnp.exp(zt - top_t[:, None])
    exp_s = jnp.exp(zs - top_s[:, None])
    sum_t, sum_s, cross = lax.psum(
        (jnp.sum(exp_t, axis=1), jnp.sum(exp_s, axis=1), jnp.sum(exp_t * (zt - zs), axis=1)),
        ("grp", "vocab"),
    )
    kl = cross / sum_t - top_t - jnp.log(sum_t) + top_s + jnp.log(sum_s)
    onehot = (domain_ids[:, None] == jnp.arange(NDOM, dtype=jnp.int32)[None, :]).astype(jnp.float32)
    counted = jnp.sum(onehot * domain_counts.astype(jnp.float32)[None, :], axis=1)
    weight = TOK / NDOM / counted
    domain_loss = jnp.sum(onehot * (weight * kl)[:, None], axis=0)
    dlogit = (weight[:, None] * (exp_s / sum_s[:, None] - exp_t / sum_t[:, None])).astype(
        jnp.bfloat16
    )
    shares = lax.psum_scatter(
        jnp.dot(dlogit, s_head, preferred_element_type=jnp.float32),
        "vocab",
        scatter_dimension=0,
        tiled=True,
    )
    grad_hidden = lax.psum_scatter(shares, "grp", scatter_dimension=1, tiled=True)
    return (grad_hidden, domain_loss)


def solution(mesh):
    return jax.shard_map(
        per_device,
        mesh=mesh,
        in_specs=(
            P(None, "vocab"),
            P("vocab", "grp"),
            P("vocab", "grp"),
            P("grp"),
            P("vocab", "grp"),
            P(("grp", "vocab"), None),
            P(("grp", "vocab"), None),
            P(),
            P(),
        ),
        out_specs=(P("vocab", "grp"), P()),
        check_vma=False,
    )
```

profile of v0, /device:TPU:1, one launch (start us, length us, event | category | flops | bytes accessed | tf_op | source)
XLA Modules:
  0.0 732.6 jit_solution(9633715813023939762)
XLA Ops:
  7.2 40.1 %all-gather = bf16[16,12,128]{2,1,0:T(8,128)(2,1)} all-gather(bf16[1,12,128]{2,1,0:T(8,128)(2,1)} %bitcast.18), channel_id=1, replica_groups=mesh['grp'=32,'vocab'=16] {'vocab'}, dimensions={0}, use_global_device_ids=true | all-gather | bytes 52224 | tf_op jit(solution)/shard_map/all_gather | solution.py:29
  48.9 2.3 fusion.13
  51.2 32.9 %fusion = f32[16,160]{1,0:T(8,128)S(1)} fusion(f32[192,160]{1,0:T(8,128)} %fusion.13), kind=kCustom, calls=%all-reduce-scatter | all-reduce-scatter fusion | flops 40961 | bytes 135168
  84.1 1.9 collective-permute-start.2
  86.0 1.9 collective-permute-start.1
  87.9 3.9 collective-permute-start
  92.4 1.9 collective-permute-start.3
  96.2 6.8 concatenate
  103.9 101.9 %psum.29 = f32[12,1]{0,1:T(1,128)S(1)} all-reduce(f32[12,1]{0,1:T(1,128)S(1)} %bitcast.19), channel_id=1, replica_groups=mesh['grp'=32,'vocab'=16] {'grp'}, use_global_device_ids=true, to_apply=%region_7.0 | all-reduce | flops 12 | bytes 96 | tf_op jit(solution)/shard_map/psum | solution.py:25
  206.6 36.6 %all-gather.1 = bf16[16,12,160]{2,1,0:T(8,128)(2,1)} all-gather(bf16[1,12,160]{2,1,0:T(8,128)(2,1)S(1)} %fusion.10), channel_id=1, replica_groups=mesh['grp'=32,'vocab'=16] {'vocab'}, dimensions={0}, use_global_device_ids=true | all-gather | bytes 65280 | tf_op jit(solution)/shard_map/all_gather | solution.py:27
  248.6 2.7 fusion.12
  251.2 80.0 %all-gather.7.cloned.1.call-done = bf16[192,5120]{0,1:T(8,128)(2,1)} async-done(((bf16[192,160]{0,1:T(8,128)(2,1)}), bf16[192,5120]{0,1:T(8,128)(2,1)}) %all-gather.7.cloned.1.call-update) | async-done | bytes 1966096 | tf_op jit(solution)/shard_map/all_gather | solution.py:28
  331.3 3.1 fusion.11
  334.4 102.9 %all-reduce.5 = (f32[192]{0:T(256)S(1)}, f32[192]{0:T(256)S(1)}) all-reduce(f32[192]{0:T(256)S(1)} %get-tuple-element.12, f32[192]{0:T(256)S(1)} %get-tuple-element.14), channel_id=1, replica_groups=mesh['grp'=32,'vocab'=16] {'grp','vocab'}, use_global_device_ids=true, to_apply=%region_9.0 | all-reduce | flops 384 | bytes 3072 | tf_op jit(solution)/shard_map/pmax | solution.py:33
  437.3 1.7 multiply_reduce_fusion
  439.0 99.5 %all-reduce.4 = (f32[192]{0:T(256)}, f32[192]{0:T(256)}, f32[192]{0:T(256)}) all-reduce(f32[192]{0:T(256)S(1)} %get-tuple-element.3, f32[192]{0:T(256)} %get-tuple-element.4, f32[192]{0:T(256)S(1)} %get-tuple-element.2), channel_id=1, replica_groups=mesh['grp'=32,'vocab'=16] {'grp','vocab'}, use_global_device_ids=true, to_apply=%region_11.0 | all-reduce | flops 576 | bytes 4608 | tf_op jit(solution)/shard_map/psum | solution.py:36
  539.2 3.3 fusion.4
  542.5 51.9 %fusion.1 = f32[16,4096]{1,0:T(8,128)S(1)} fusion(f32[192,4096]{1,0:T(8,128)} %fusion.4), kind=kCustom, calls=%all-reduce-scatter.1 | all-reduce-scatter fusion | flops 1048577 | bytes 3409920
  595.8 3.3 collective-permute-start.5
  599.0 3.3 collective-permute-start.4
  602.4 1.8 collective-permute-start.7
  604.2 3.3 collective-permute-done.7
  609.0 7.2 concatenate.1
  617.6 108.5 %reduce-scatter.6.cloned.1.call-done = f32[12,128]{1,0:T(8,128)} async-done(((f32[12,4096]{1,0:T(8,128)}), f32[12,128]{1,0:T(8,128)}) %reduce-scatter.6.cloned.1.call-update) | async-done | bytes 6160 | tf_op jit(solution)/shard_map/reduce_scatter | solution.py:54
  (41 shorter events, 15.3 us)
Async XLA Ops:
  7.2 324.1 %copy-start = (bf16[192,5120]{1,0:T(8,128)(2,1)S(1)}, bf16[192,5120]{1,0:T(8,128)(2,1)}, u32[]{:S(2)}) copy-start(bf16[192,5120]{1,0:T(8,128)(2,1)} %param.14) | copy-start | bytes 5898244
  7.2 241.4 %copy-start.1 = (bf16[192,4096]{1,0:T(8,128)(2,1)S(1)}, bf16[192,4096]{1,0:T(8,128)(2,1)}, u32[]{:S(2)}) copy-start(bf16[192,4096]{1,0:T(8,128)(2,1)} %param.15) | copy-start | bytes 4718596
  7.2 241.4 %all-gather.5.cloned.1.call-start = ((), (), s32[]{:S(2)}) async-start(), calls=%async_computation.1 | async-start | bytes 1622016 | tf_op jit(solution)/shard_map/all_gather | solution.py:30
  48.9 282.4 %all-gather.7.cloned.1.call-start = ((), (), s32[]{:S(2)}) async-start(), calls=%async_computation.2 | async-start | bytes 2703360 | tf_op jit(solution)/shard_map/all_gather | solution.py:28
  84.1 12.1 %collective-permute-start.2 = (f32[16,160]{1,0:T(8,128)S(1)}, f32[16,160]{1,0:T(8,128)}, u32[]{:S(2)}, u32[]{:S(2)}) collective-permute-start(f32[16,160]{1,0:T(8,128)S(1)} %fusion), channel_id=1, source_target_pairs={{0,3},{1,4},{2,5},{3,6},{4,7},{5,8},{6,9},{7,10},{8,11},{9,12},{10... | collective-permute-start | bytes 30728
  86.0 10.2 %collective-permute-start.1 = (f32[16,160]{1,0:T(8,128)S(1)}, f32[16,160]{1,0:T(8,128)}, u32[]{:S(2)}, u32[]{:S(2)}) collective-permute-start(f32[16,160]{1,0:T(8,128)S(1)} %fusion), channel_id=1, source_target_pairs={{0,2},{1,3},{2,4},{3,5},{4,6},{5,7},{6,8},{7,9},{8,10},{9,11},{10,... | collective-permute-start | bytes 30728
  87.9 8.3 %collective-permute-start = (f32[16,160]{1,0:T(8,128)S(1)}, f32[16,160]{1,0:T(8,128)}, u32[]{:S(2)}, u32[]{:S(2)}) collective-permute-start(f32[16,160]{1,0:T(8,128)S(1)} %fusion), channel_id=1, source_target_pairs={{0,1},{1,2},{2,3},{3,4},{4,5},{5,6},{6,7},{7,8},{8,9},{9,10},{10,1... | collective-permute-start | bytes 30728
  92.4 3.8 collective-permute-start.3
  246.5 479.6 %reduce-scatter.6.cloned.1.call-start = ((), (), s32[]{:S(2)}) async-start(), calls=%async_computation.3 | async-start | bytes 270336 | tf_op jit(solution)/shard_map/reduce_scatter | solution.py:54
  594.4 22.5 %copy-start.5 = (s32[192]{0:T(256)S(1)}, s32[192]{0:T(256)}, u32[]{:S(2)}) copy-start(s32[192]{0:T(256)} %param.16) | copy-start | bytes 2308
  594.4 13.1 %collective-permute-start.6 = (f32[16,4096]{1,0:T(8,128)S(1)}, f32[16,4096]{1,0:T(8,128)S(1)}, u32[]{:S(2)}, u32[]{:S(2)}) collective-permute-start(f32[16,4096]{1,0:T(8,128)S(1)} %fusion.1), channel_id=1, source_target_pairs={{0,3},{1,4},{2,5},{3,6},{4,7},{5,8},{6,9},{7,10},{8,11},{9,12},{10... | collective-permute-start | bytes 786440
  595.8 11.7 %collective-permute-start.5 = (f32[16,4096]{1,0:T(8,128)S(1)}, f32[16,4096]{1,0:T(8,128)S(1)}, u32[]{:S(2)}, u32[]{:S(2)}) collective-permute-start(f32[16,4096]{1,0:T(8,128)S(1)} %fusion.1), channel_id=1, source_target_pairs={{0,2},{1,3},{2,4},{3,5},{4,6},{5,7},{6,8},{7,9},{8,10},{9,11},{10,... | collective-permute-start | bytes 786440
  599.0 10.0 %collective-permute-start.4 = (f32[16,4096]{1,0:T(8,128)S(1)}, f32[16,4096]{1,0:T(8,128)}, u32[]{:S(2)}, u32[]{:S(2)}) collective-permute-start(f32[16,4096]{1,0:T(8,128)S(1)} %fusion.1), channel_id=1, source_target_pairs={{0,1},{1,2},{2,3},{3,4},{4,5},{5,6},{6,7},{7,8},{8,9},{9,10},{10,1... | collective-permute-start | bytes 786440
  602.4 5.1 collective-permute-start.7
  607.5 0.7 copy-start.4
  607.5 0.8 copy-start.2
  608.3 0.7 copy-start.3
Sparse Core Ops, SparseCore 0:
  49.0 84.3 all-gather.4
  246.6 84.6 all-gather.6
  617.0 108.9 reduce-scatter.5
where the time goes:
time: 735 us; the launch traced here: 733 us
  blocking collectives  466 us (63%)
  waiting for transfers between devices  192 us (26%)
  local copies, waits for them, and re-layouts  22.8 us (3%)
  starting transfers between devices  19.4 us (3%)
  between operations  14.5 us (2%)
  matrix products  11.4 us (2%)
    reduce_scatter x1, waiting for transfers between devices, per_device(): lax.psum_scatter(shares, 'grp', scatter_dimension=1, tiled=True)  109 us
    pmax x1, blocking collectives, per_device(): top_t, top_s = lax.pmax((local_t, local_s), ('grp', 'vocab'))  103 us
    psum x1, blocking collectives, per_device(): squares = lax.psum(jnp.sum(pre * pre, axis=1, keepdims=True), 'grp')  102 us
    psum x1, blocking collectives, per_device(): lax.psum((jnp.sum(exp_t, axis=1), jnp.sum(exp_s, axis=1), jnp.sum(exp_t *...  99.5 us
    unnamed x2, blocking collectives  84.8 us
    all_gather x1, waiting for transfers between devices, per_device(): zt = folding(t_head, lax.all_gather(t_rows, 'grp', axis=1, tiled=True))  80 us
    all_gather x1, blocking collectives, per_device(): s_rows = lax.all_gather(s_hidden, 'vocab', axis=0, tiled=True)  40.1 us
    all_gather x1, blocking collectives, per_device(): t_rows = lax.all_gather(t_norm, 'vocab', axis=0, tiled=True)  36.6 us
  transfers between devices with their start and end apart: 11, of which 3 were waited for; matrix products, arithmetic and copies ran while one was open for 7% of the time, Pallas kernels for 0%

commit v1 on v0

v1 whole, which is shorter than its diff:
```python
import jax
import jax.numpy as jnp
from jax import lax
from jax.experimental import pallas as pl
from jax.experimental.pallas import tpu as pltpu
from jax.sharding import PartitionSpec as P

DT = 5120
DS = 4096
TOK = 192
NDOM = 8
F32 = jnp.float32
BF16 = jnp.bfloat16
MESH = pl.DeviceIdType.MESH
NSEM = 160
NT = (((1,), (1,)), ((), ()))
TN = (((0,), (0,)), ((), ()))


def iota(shape, axis):
    return lax.broadcasted_iota(jnp.int32, shape, axis)


class Links:
    def __init__(self, send, recv):
        self.send, self.recv, self.used, self.all = send, recv, 0, []

    def start(self, src, dst, device):
        k = self.used
        self.used += 1
        copy = pltpu.make_async_remote_copy(
            src_ref=src, dst_ref=dst, send_sem=self.send.at[k], recv_sem=self.recv.at[k],
            device_id=device, device_id_type=MESH,
        )
        copy.start()
        self.all.append(copy)
        return copy

    def finish(self):
        for copy in self.all:
            copy.wait_send()


def arrived(copies):
    for copy in copies:
        copy.wait_recv()


def merge(parts):
    mt, ms = parts[0][0:1], parts[0][3:4]
    for p in parts[1:]:
        mt, ms = jnp.maximum(mt, p[0:1]), jnp.maximum(ms, p[3:4])
    st = at = ss = None
    for p in parts:
        ft, fs = jnp.exp(p[0:1] - mt), jnp.exp(p[3:4] - ms)
        a, b, d = p[1:2] * ft, p[2:3] * ft, p[4:5] * fs
        st, at, ss = (a, b, d) if st is None else (st + a, at + b, ss + d)
    return mt, st, at, ms, ss


def put_stats(ref, stats):
    for row, value in enumerate(stats):
        ref[row : row + 1, :] = value


def body(
    act_hbm, down_hbm, resid_hbm, gain_hbm, hid_hbm, thead_hbm, shead_hbm, ids_hbm, counts,
    grad_out, loss_out,
    act, down, resid, gain, hid, thead, shead, ids,
    pmain, prem, ppack, psend, precv, pk, rem, rs, gs, u1, u2,
    hp, tz, tg, sg, q1, q2, q3,
    gsend, grecv, gown, gx, rxa, ryb, rya, rxb, sa, sb, fin, fsend, rzl, zsend, rzh,
    load_sem, send_sem, recv_sem,
):
    g, v = lax.axis_index("grp"), lax.axis_index("vocab")
    zh, y, c = g // 8, (g // 2) % 4, g % 2
    zl, x = v // 4, v % 4
    q = g % 8

    def at_x(d):
        return (g, zl * 4 + (x + d) % 4)

    def at_y(d):
        return (zh * 8 + ((y + d) % 4) * 2 + c, v)

    def at_zl(d):
        return (g, ((zl + d) % 4) * 4 + x)

    def at_zh(d):
        return (((zh + d) % 4) * 8 + q, v)

    def at_v(d):
        return (g, (v + d) % 16)

    def at_q(d):
        return (zh * 8 + (q + d) % 8, v)

    sibling = (zh * 8 + y * 2 + (1 - c), v)

    loads = {}
    for k, (name, src, dst) in enumerate((
        ("hid", hid_hbm, hid), ("act", act_hbm, act), ("down", down_hbm, down), ("resid", resid_hbm, resid),
        ("gain", gain_hbm, gain), ("ids", ids_hbm, ids), ("thead", thead_hbm, thead), ("shead", shead_hbm, shead),
    )):
        loads[name] = pltpu.make_async_copy(src, dst, load_sem.at[k])
        loads[name].start()

    barrier = pltpu.get_barrier_semaphore()
    for d in range(1, 16):
        pl.semaphore_signal(barrier, inc=1, device_id=at_v(d), device_id_type=MESH)
    for d in range(1, 8):
        pl.semaphore_signal(barrier, inc=1, device_id=at_q(d), device_id_type=MESH)
    for d in range(1, 4):
        pl.semaphore_signal(barrier, inc=1, device_id=at_zh(d), device_id_type=MESH)

    links = Links(send_sem, recv_sem)

    loads["hid"].wait()
    mine = sg.at[c, y, x, zl, zh]
    mine[...] = jnp.zeros((16, 128), BF16)
    mine[0:12, :] = hid[...]

    loads["act"].wait()
    loads["down"].wait()
    part = jnp.dot(act[...], down[...], preferred_element_type=F32)
    pmain[...] = part[:, 0:128]
    prem[:, 0:32] = part[:, 128:160]
    lane48 = iota((48, 128), 1) // 32
    packed = jnp.zeros((48, 128), F32)
    for k in range(4):
        rows = prem[pl.ds(k, 48, stride=4), :]
        rows = rows if k == 0 else pltpu.roll(rows, 32 * k, 1)
        packed = jnp.where(lane48 == k, rows, packed)
    ppack[...] = packed
    for vv in range(16):
        psend[vv, 0:12, :] = pmain[12 * vv : 12 * vv + 12, :]
        psend[vv, 12:15, :] = ppack[3 * vv : 3 * vv + 3, :]
        psend[vv, 15:16, :] = jnp.zeros((1, 128), F32)

    pl.semaphore_wait(barrier, 25)

    sums = [links.start(psend.at[(v + d) % 16], precv.at[d - 1], at_v(d)) for d in range(1, 16)]
    s_zh = [links.start(mine, mine, at_zh(d)) for d in range(1, 4)]

    loads["resid"].wait()
    loads["gain"].wait()
    rs[...] = jnp.zeros((16, 256), F32)
    rs[0:12, 0:160] = resid[...].astype(F32)
    gs[...] = jnp.zeros((1, 256), F32)
    gs[:, 0:160] = gain[...]
    rem[...] = jnp.zeros((16, 128), F32)

    arrived(s_zh)
    run = sg.at[c, y, x, zl]
    s_zl = [links.start(run, run, at_zl(d)) for d in range(1, 4)]

    arrived(sums)
    total = psend[v]
    for d in range(15):
        total = total + precv[d]
    pk[...] = total
    for k in range(4):
        rows = total[12:15, :] if k == 0 else pltpu.roll(total, 128 - 32 * k, 1)[12:15, :]
        for j in range(3):
            rem[4 * j + k : 4 * j + k + 1, 0:32] = rows[j : j + 1, 0:32]
    pre_a = jnp.where(iota((16, 128), 0) < 12, total, 0.0) + rs[:, 0:128]
    pre_b = rem[...] + rs[:, 128:256]
    diagonal = iota((16, 128), 0) == iota((16, 128), 1)
    column = jnp.sum(pre_a * pre_a + pre_b * pre_b, axis=1, keepdims=True)
    u1[q] = jnp.sum(jnp.where(diagonal, column, 0.0), axis=0, keepdims=True)
    squares = [links.start(u1.at[q], u1.at[q], at_q(d)) for d in range(1, 8)]

    def spread(buf, lo, hi):
        one = buf.at[c, y, x, pl.ds(0, 2)]
        two = buf.at[c, y, x, pl.ds(2, 2)]
        a = [links.start(one, one, at_x(d)) for d in range(1, 4)]
        b = [links.start(two, two, at_y(d)) for d in range(1, 4)]
        return a, b

    def spread_on(buf):
        one = buf.at[c, y, :, pl.ds(0, 2)]
        two = buf.at[c, :, x, pl.ds(2, 2)]
        a = [links.start(one, one, at_y(d)) for d in range(1, 4)]
        b = [links.start(two, two, at_x(d)) for d in range(1, 4)]
        return a, b, [links.start(one, one, sibling), links.start(two, two, sibling)]

    def hand_over(buf, a, b, core):
        for d in range(1, 4):
            a[d - 1].wait_recv()
            one = buf.at[c, (y + 4 - d) % 4, :, pl.ds(0, 2)]
            core.append(links.start(one, one, sibling))
            b[d - 1].wait_recv()
            two = buf.at[c, :, (x + 4 - d) % 4, pl.ds(2, 2)]
            core.append(links.start(two, two, sibling))

    arrived(s_zl)
    s_a, s_b = spread(sg, 0, 2)

    arrived(squares)
    line = u1[0]
    for k in range(1, 8):
        line = line + u1[k]
    u2[zh] = line
    squares = [links.start(u2.at[zh], u2.at[zh], at_zh(d)) for d in range(1, 4)]

    arrived(squares)
    line = (u2[0] + u2[1]) + (u2[2] + u2[3])
    column = jnp.sum(jnp.where(diagonal, line, 0.0), axis=1, keepdims=True)
    scale = lax.rsqrt(column / DT + 1e-06)
    norm_a = pre_a * scale * gs[:, 0:128]
    norm_b = pre_b * scale * gs[:, 128:256]
    moved = norm_b
    for h in range(1, 4):
        moved = jnp.where(zh == h, pltpu.roll(norm_b, 32 * h, 1), moved)
    tz[zh, 0] = norm_a.astype(BF16)
    tz[zh, 1] = moved.astype(BF16)
    t_zh = [links.start(tz.at[zh], tz.at[zh], at_zh(d)) for d in range(1, 4)]

    arrived(s_a)
    arrived(s_b)
    s_a, s_b, s_core = spread_on(sg)

    arrived(t_zh)
    for h in range(4):
        tg[c, y, x, zl, h] = tz[h, 0]
    tg[c, y, x, zl, 4] = ((tz[0, 1].astype(F32) + tz[1, 1].astype(F32)) + (tz[2, 1].astype(F32) + tz[3, 1].astype(F32))).astype(BF16)
    run = tg.at[c, y, x, zl]
    t_zl = [links.start(run, run, at_zl(d)) for d in range(1, 4)]

    hand_over(sg, s_a, s_b, s_core)

    arrived(t_zl)
    t_a, t_b = spread(tg, 0, 2)

    loads["thead"].wait()
    lane = iota((192, 128), 1)
    for qq in range(8):
        last = jnp.zeros((192, 128), F32)
        off = 32 * (qq % 4)
        for h in range(4):
            first = ((h * 8 + qq) * 160) // 128
            right = thead[:, (first + 1) * 128 : (first + 2) * 128].astype(F32)
            if off == 0:
                hp[qq, h] = thead[:, first * 128 : (first + 1) * 128]
            else:
                left = thead[:, first * 128 : (first + 1) * 128].astype(F32)
                joined = jnp.where(lane < off, right, left)
                hp[qq, h] = pltpu.roll(joined, 128 - off, 1).astype(BF16)
            shift = (32 * h - off) % 128
            moved = right if shift == 0 else pltpu.roll(right, shift, 1)
            last = jnp.where(lane // 32 == h, moved, last)
        hp[qq, 4] = last.astype(BF16)

    arrived(t_a)
    arrived(t_b)
    t_a, t_b, t_core = spread_on(tg)
    hand_over(tg, t_a, t_b, t_core)

    def rows_of(buf, cc, yy, j):
        return buf[cc, yy, :, :, j].reshape(256, 128)

    def student(cc, acc):
        for yy in range(4):
            left = jnp.concatenate(
                [shead[:, pl.ds(pl.multiple_of((h * 8 + yy * 2 + cc) * 128, 128), 128)] for h in range(4)], axis=1)
            right = jnp.concatenate([rows_of(sg, cc, yy, h) for h in range(4)], axis=1)
            one = lax.dot_general(left, right, NT, preferred_element_type=F32)
            acc = one if acc is None else acc + one
        return acc

    def teacher(cc, acc):
        for yy in range(4):
            left = jnp.concatenate([hp[yy * 2 + cc, j] for j in range(5)], axis=1)
            right = jnp.concatenate([rows_of(tg, cc, yy, j) for j in range(5)], axis=1)
            one = lax.dot_general(left, right, NT, preferred_element_type=F32)
            acc = one if acc is None else acc + one
        return acc

    loads["shead"].wait()
    zs = student(c, None)
    arrived(s_core)
    zs = student(1 - c, zs)
    zt = teacher(c, None)
    arrived(t_core)
    zt = teacher(1 - c, zt)

    mt = jnp.max(zt, axis=0, keepdims=True)
    ms = jnp.max(zs, axis=0, keepdims=True)
    et = jnp.exp(zt - mt)
    stats = (
        mt,
        jnp.sum(et, axis=0, keepdims=True),
        jnp.sum(et * (zt - zs), axis=0, keepdims=True),
        ms,
        jnp.sum(jnp.exp(zs - ms), axis=0, keepdims=True),
    )
    blank = jnp.zeros((8, 256), F32)
    for buf, slot, count, peer in ((q1, v, 16, at_v), (q2, q, 8, at_q), (q3, zh, 4, at_zh)):
        own = buf.at[slot]
        own[...] = blank
        put_stats(own, stats)
        arrived([links.start(own, own, peer(d)) for d in range(1, count)])
        stats = merge([buf[k] for k in range(count)])
    mt, st, at, ms, ss = stats

    loads["ids"].wait()
    spot = iota((192, 256), 1)
    token = ((spot // 16) % 4 * 4 + spot // 64) * 12 + spot % 16
    chosen = jnp.where((token == iota((192, 256), 0)) & (spot % 16 < 12), 1.0, 0.0).astype(BF16)
    domain = jnp.dot(
        jnp.broadcast_to(ids[...], (8, 192)).astype(F32).astype(BF16), chosen, preferred_element_type=F32)[0:1]
    counted = jnp.zeros((1, 256), F32)
    for k in range(NDOM):
        counted = jnp.where(domain == float(k), counts[k].astype(F32), counted)
    weight = TOK / NDOM / counted

    dl = (jnp.exp(zs - ms) * (weight / ss) - jnp.exp(zt - mt) * (weight / st)).astype(BF16)

    def blocks(cc, yy):
        right = jnp.concatenate(
            [shead[:, pl.ds(pl.multiple_of((h * 8 + yy * 2 + cc) * 128, 128), 128)] for h in range(4)], axis=1)
        return lax.dot_general(dl, right, TN, preferred_element_type=F32)

    over = []
    for yy in range(4):
        piece = blocks(1 - c, yy)
        for h in range(4):
            gsend[yy, :, :, h] = piece[:, h * 128 : h * 128 + 128].astype(BF16).reshape(4, 4, 16, 128)
        over.append(links.start(gsend.at[yy], grecv.at[yy], sibling))
    for yy in range(4):
        piece = blocks(c, yy)
        for h in range(4):
            gown[yy, :, :, h] = piece[:, h * 128 : h * 128 + 128].reshape(4, 4, 16, 128)

    kl = at / st - mt - jnp.log(st) + ms + jnp.log(ss)
    real = iota((1, 256), 1) % 16 < 12
    loss = jnp.zeros((1, NDOM), F32)
    for k in range(NDOM):
        one = jnp.sum(jnp.where(real & (domain == float(k)), weight * kl, 0.0), axis=1, keepdims=True)
        loss = jnp.where(iota((1, NDOM), 1) == k, one, loss)
    loss_out[...] = loss

    for yy in range(4):
        over[yy].wait_recv()
        both = gown[yy] + grecv[yy].astype(F32)
        gown[yy] = both
        gx[yy] = both.astype(BF16)
    r_a = [links.start(gx.at[:, (x + d) % 4, pl.ds(0, 2)], rxa.at[d - 1], at_x(d)) for d in range(1, 4)]
    r_b = [links.start(gx.at[(y + d) % 4, :, pl.ds(2, 2)], ryb.at[d - 1], at_y(d)) for d in range(1, 4)]

    arrived(r_a)
    acc = gown[:, x, 0:2]
    for d in range(3):
        acc = acc + rxa[d].astype(F32)
    gown[:, x, 0:2] = acc
    sa[...] = acc.astype(BF16)
    r_a = [links.start(sa.at[(y + d) % 4], rya.at[d - 1], at_y(d)) for d in range(1, 4)]
    arrived(r_b)
    acc = gown[y, :, 2:4]
    for d in range(3):
        acc = acc + ryb[d].astype(F32)
    gown[y, :, 2:4] = acc
    sb[...] = acc.astype(BF16)
    r_b = [links.start(sb.at[(x + d) % 4], rxb.at[d - 1], at_x(d)) for d in range(1, 4)]

    arrived(r_a)
    acc = gown[y, x, 0:2]
    for d in range(3):
        acc = acc + rya[d].astype(F32)
    fin[0:2] = acc
    fsend[0:2] = acc.astype(BF16)
    arrived(r_b)
    acc = gown[y, x, 2:4]
    for d in range(3):
        acc = acc + rxb[d].astype(F32)
    fin[2:4] = acc
    fsend[2:4] = acc.astype(BF16)
    arrived([links.start(fsend.at[(zl + d) % 4], rzl.at[d - 1], at_zl(d)) for d in range(1, 4)])
    acc = fin[zl]
    for d in range(3):
        acc = acc + rzl[d].astype(F32)
    fin[0] = acc
    zsend[...] = acc.astype(BF16)
    arrived([links.start(zsend.at[(zh + d) % 4], rzh.at[d - 1], at_zh(d)) for d in range(1, 4)])
    acc = fin[0, zh]
    for d in range(3):
        acc = acc + rzh[d].astype(F32)
    grad_out[...] = acc[0:12, :]
    links.finish()


def per_device(t_act, t_down, t_resid, t_gain, s_hidden, t_head, s_head, domain_ids, domain_counts):
    anywhere = pl.BlockSpec(memory_space=pl.ANY)
    held = pl.BlockSpec(memory_space=pltpu.VMEM)

    def vmem(shape, dtype=F32):
        return pltpu.VMEM(shape, dtype)

    grad, loss = pl.pallas_call(
        body,
        out_shape=(jax.ShapeDtypeStruct((12, 128), F32), jax.ShapeDtypeStruct((1, NDOM), F32)),
        in_specs=[anywhere] * 8 + [pl.BlockSpec(memory_space=pltpu.SMEM)],
        out_specs=(held, held),
        scratch_shapes=[
            vmem((192, 1600), BF16), vmem((1600, 160), BF16), vmem((12, 160), BF16), vmem((1, 160)),
            vmem((12, 128), BF16), vmem((192, DT), BF16), vmem((192, DS), BF16), vmem((1, TOK), jnp.int32),
            vmem((192, 128)), vmem((192, 128)), vmem((48, 128)),
            vmem((16, 16, 128)), vmem((15, 16, 128)), vmem((16, 128)), vmem((16, 128)),
            vmem((16, 256)), vmem((1, 256)), vmem((8, 1, 128)), vmem((4, 1, 128)),
            vmem((8, 5, 192, 128), BF16), vmem((4, 2, 16, 128), BF16),
            vmem((2, 4, 4, 4, 5, 16, 128), BF16), vmem((2, 4, 4, 4, 4, 16, 128), BF16),
            vmem((16, 8, 256)), vmem((8, 8, 256)), vmem((4, 8, 256)),
            vmem((4, 4, 4, 4, 16, 128), BF16), vmem((4, 4, 4, 4, 16, 128), BF16),
            vmem((4, 4, 4, 4, 16, 128)), vmem((4, 4, 4, 4, 16, 128), BF16),
            vmem((3, 4, 2, 4, 16, 128), BF16), vmem((3, 4, 2, 4, 16, 128), BF16),
            vmem((3, 2, 4, 16, 128), BF16), vmem((3, 2, 4, 16, 128), BF16),
            vmem((4, 2, 4, 16, 128), BF16), vmem((4, 2, 4, 16, 128), BF16),
            vmem((4, 4, 16, 128)), vmem((4, 4, 16, 128), BF16), vmem((3, 4, 16, 128), BF16),
            vmem((4, 16, 128), BF16), vmem((3, 16, 128), BF16),
            pltpu.SemaphoreType.DMA((8,)), pltpu.SemaphoreType.DMA((NSEM,)), pltpu.SemaphoreType.DMA((NSEM,)),
        ],
        compiler_params=pltpu.CompilerParams(
            collective_id=0, has_side_effects=True, vmem_limit_bytes=44 * 1024 * 1024),
    )(
        t_act, t_down, t_resid, t_gain.reshape(1, -1), s_hidden, t_head, s_head, domain_ids.reshape(1, -1),
        domain_counts,
    )
    return grad, loss.reshape(NDOM)


def solution(mesh):
    return jax.shard_map(
        per_device,
        mesh=mesh,
        in_specs=(
            P(None, "vocab"),
            P("vocab", "grp"),
            P("vocab", "grp"),
            P("grp"),
            P("vocab", "grp"),
            P(("grp", "vocab"), None),
            P(("grp", "vocab"), None),
            P(),
            P(),
        ),
        out_specs=(P("vocab", "grp"), P()),
        check_vma=False,
    )
```

time: 735 us -> 118 us (0.16)
  blocking collectives: 466 us -> 0 us
  waiting for transfers between devices: 192 us -> 0 us
  Pallas kernels: 0 us -> 107 us
  starting transfers between devices: 19.4 us -> 0 us
  between operations: 14.5 us -> 0.66 us
  local copies, waits for them, and re-layouts: 22.8 us -> 9.87 us
  matrix products: 11.4 us -> 0 us
    psum x2 -> x0, blocking collectives: 201 us -> none  [the longest x1 102 us: per_device(): squares = lax.psum(jnp.sum(pre * pre, axis=1, keepdims=True), 'grp')]
    reduce_scatter x1 -> x0, waiting for transfers between devices: 109 us -> none  [per_device(): lax.psum_scatter(shares, 'grp', scatter_dimension=1, tiled=True)]
    pallas_call x0 -> x1, Pallas kernels: none -> 107 us  [per_device(): pl.pallas_call(body, out_shape=(jax.ShapeDtypeStruct((12, 128), F32), jax...]
    pmax x1 -> x0, blocking collectives: 103 us -> none  [per_device(): top_t, top_s = lax.pmax((local_t, local_s), ('grp', 'vocab'))]
    unnamed x2 -> x0, blocking collectives: 84.8 us -> none
    all_gather x2 -> x0, waiting for transfers between devices: 80 us -> none  [the longest x1 80 us: per_device(): zt = folding(t_head, lax.all_gather(t_rows, 'grp', axis=1, tiled=True))]
    all_gather x2 -> x0, blocking collectives: 76.8 us -> none  [the longest x1 40.1 us: per_device(): s_rows = lax.all_gather(s_hidden, 'vocab', axis=0, tiled=True)]
    unnamed x8 -> x0, starting transfers between devices: 19.2 us -> none
  transfers between devices with their start and end apart: 11 -> 0, of which waited for: 3 -> 0; matrix products, arithmetic and copies ran while one was open for 7% -> 0% of each run, Pallas kernels for 0% -> 0%
where the time goes in v1:
time: 118 us; the launch traced here: 117 us
  Pallas kernels  107 us (91%)
  local copies, waits for them, and re-layouts  9.87 us (8%)
    pallas_call x1, Pallas kernels, per_device(): pl.pallas_call(body, out_shape=(jax.ShapeDtypeStruct((12, 128), F32), jax...  107 us
    unnamed x19, local copies, waits for them, and re-layouts  9.87 us

profile of v1, /device:TPU:1, one launch (start us, length us, event | category | flops | bytes accessed | tf_op | source)
XLA Modules:
  0.0 117.3 jit_solution(14943485218358471097)
XLA Ops:
  0.6 1.3 %copy.11.down_hbm = bf16[1600,160]{1,0:T(8,128)(2,1)S(1)} copy(bf16[1600,160]{0,1:T(8,128)(2,1)} %param.10) | data formatting | bytes 1024000 | tf_op args[1]
  2.0 0.0 copy-start
  2.0 1.5 %copy-done = bf16[192,5120]{1,0:T(8,128)(2,1)S(1)} copy-done((bf16[192,5120]{1,0:T(8,128)(2,1)S(1)}, bf16[192,5120]{1,0:T(8,128)(2,1)}, u32[]{:S(2)}) %copy-start) | copy-done | bytes 1966104
  3.5 0.0 copy-start.1
  3.5 1.4 %copy-done.1 = bf16[192,4096]{1,0:T(8,128)(2,1)S(1)} copy-done((bf16[192,4096]{1,0:T(8,128)(2,1)S(1)}, bf16[192,4096]{1,0:T(8,128)(2,1)}, u32[]{:S(2)}) %copy-start.1) | copy-done | bytes 1572888
  4.9 0.0 copy-start.2
  4.9 1.1 copy-done.2
  6.0 0.0 copy-start.3
  6.0 0.7 copy-done.3
  6.7 0.0 copy-start.4
  6.7 0.7 copy-done.4
  7.4 0.0 copy-start.5
  7.4 0.7 copy-done.5
  8.1 0.0 copy-start.6
  8.1 0.7 copy-done.6
  8.7 0.0 copy-start.7
  8.7 0.7 copy-done.7
  9.4 106.8 %shard_map.104 = (f32[12,128]{1,0:T(8,128)S(1)}, f32[1,8]{1,0:T(1,128)S(1)}) custom-call(bf16[192,1600]{1,0:T(8,128)(2,1)S(1)} %copy-done.2, bf16[1600,160]{1,0:T(8,128)(2,1)S(1)} %copy.11.down_hbm, bf16[12,160]{1,0:T(8,128)(2,1)S(1)} %copy-done.3, f32[1,160]{1,0:T(1,128)S(1)} %bitcast.3, bf16[12,128]{1,0:T(8,128)(2,1)S(1)} %copy-done.4, ...), custom_call_target="tpu_custom_call" | custom-call | tf_op jit(solution)/shard_map/pallas_call | solution.py:399
  116.2 0.6 copy.14
  116.8 0.5 copy.15
Async XLA Ops:
  2.0 1.5 %copy-start = (bf16[192,5120]{1,0:T(8,128)(2,1)S(1)}, bf16[192,5120]{1,0:T(8,128)(2,1)}, u32[]{:S(2)}) copy-start(bf16[192,5120]{1,0:T(8,128)(2,1)} %thead_hbm.1) | copy-start | bytes 5898244
  3.5 1.4 %copy-start.1 = (bf16[192,4096]{1,0:T(8,128)(2,1)S(1)}, bf16[192,4096]{1,0:T(8,128)(2,1)}, u32[]{:S(2)}) copy-start(bf16[192,4096]{1,0:T(8,128)(2,1)} %shead_hbm.1) | copy-start | bytes 4718596
  4.9 1.1 copy-start.2
  6.0 0.7 copy-start.3
  6.7 0.7 copy-start.4
  7.4 0.7 copy-start.5
  8.1 0.7 copy-start.6
  8.7 0.7 copy-start.7

commit v2 on v1

v2 whole, which is shorter than its diff:
```python
import jax
import jax.numpy as jnp
from jax import lax
from jax.experimental import pallas as pl
from jax.experimental.pallas import tpu as pltpu
from jax.sharding import PartitionSpec as P

DT = 5120
DS = 4096
TOK = 192
NDOM = 8
F32 = jnp.float32
BF16 = jnp.bfloat16
MESH = pl.DeviceIdType.MESH
NSEM = 160
NT = (((1,), (1,)), ((), ()))


def iota(shape, axis):
    return lax.broadcasted_iota(jnp.int32, shape, axis)


class Links:
    def __init__(self, send, recv):
        self.send, self.recv, self.used, self.all = send, recv, 0, []

    def start(self, src, dst, device):
        k = self.used
        self.used += 1
        copy = pltpu.make_async_remote_copy(
            src_ref=src, dst_ref=dst, send_sem=self.send.at[k], recv_sem=self.recv.at[k],
            device_id=device, device_id_type=MESH,
        )
        copy.start()
        self.all.append(copy)
        return copy

    def finish(self):
        for copy in self.all:
            copy.wait_send()


def arrived(copies):
    for copy in copies:
        copy.wait_recv()


def merge(buf, count):
    mt, ms = buf[0, 0], buf[0, 3]
    for k in range(1, count):
        mt, ms = jnp.maximum(mt, buf[k, 0]), jnp.maximum(ms, buf[k, 3])
    st = at = ss = jnp.zeros((1, 256), F32)
    for k in range(count):
        ft, fs = jnp.exp(buf[k, 0] - mt), jnp.exp(buf[k, 3] - ms)
        st, at, ss = st + buf[k, 1] * ft, at + buf[k, 2] * ft, ss + buf[k, 4] * fs
    return mt, st, at, ms, ss


def body(
    act_hbm, down_hbm, resid_hbm, gain_hbm, hid_hbm, thead_hbm, shead_hbm, ids_hbm, counts_hbm,
    grad_out, loss_out,
    act, down, resid, gain, hid, thead, shead, ids, counts,
    pmain, prem, ppack, psend, precv, rem, rs, gs, u1, u2,
    hp, tz, tg, sg, q1, q2, q3,
    gsend, grecv, gown, gx, rxa, ryb, rya, rxb, sa, sb, fin, fsend, rzl, zsend, rzh,
    load_sem, send_sem, recv_sem,
):
    g, v = lax.axis_index("grp"), lax.axis_index("vocab")
    zh, y, c = g // 8, (g // 2) % 4, g % 2
    zl, x = v // 4, v % 4
    q = g % 8

    def at_x(d):
        return (g, zl * 4 + (x + d) % 4)

    def at_y(d):
        return (zh * 8 + ((y + d) % 4) * 2 + c, v)

    def at_zl(d):
        return (g, ((zl + d) % 4) * 4 + x)

    def at_zh(d):
        return (((zh + d) % 4) * 8 + q, v)

    def at_v(d):
        return (g, (v + d) % 16)

    def at_q(d):
        return (zh * 8 + (q + d) % 8, v)

    sibling = (zh * 8 + y * 2 + (1 - c), v)

    loads = {}
    for k, (name, src, dst) in enumerate((
        ("hid", hid_hbm, hid), ("act", act_hbm, act), ("down", down_hbm, down), ("resid", resid_hbm, resid),
        ("gain", gain_hbm, gain), ("ids", ids_hbm, ids), ("counts", counts_hbm, counts), ("thead", thead_hbm, thead),
        ("shead", shead_hbm, shead),
    )):
        loads[name] = pltpu.make_async_copy(src, dst, load_sem.at[k])
        loads[name].start()

    barrier = pltpu.get_barrier_semaphore()
    for d in range(1, 16):
        pl.semaphore_signal(barrier, inc=1, device_id=at_v(d), device_id_type=MESH)
    for d in range(1, 8):
        pl.semaphore_signal(barrier, inc=1, device_id=at_q(d), device_id_type=MESH)
    for d in range(1, 4):
        pl.semaphore_signal(barrier, inc=1, device_id=at_zh(d), device_id_type=MESH)

    links = Links(send_sem, recv_sem)

    loads["hid"].wait()
    mine = sg.at[c, y, x, zl, zh]
    mine[...] = jnp.zeros((16, 128), BF16)
    mine[0:12, :] = hid[...]

    pl.semaphore_wait(barrier, 25)
    s_zh = [links.start(mine, mine, at_zh(d)) for d in range(1, 4)]

    loads["act"].wait()
    loads["down"].wait()
    part = lax.dot_general(act[...], down[...], NT, preferred_element_type=F32)
    pmain[...] = part[:, 0:128]
    prem[:, 0:32] = part[:, 128:160]
    lane48 = iota((48, 128), 1) // 32
    packed = jnp.zeros((48, 128), F32)
    for k in range(4):
        rows = prem[pl.ds(k, 48, stride=4), :]
        rows = rows if k == 0 else pltpu.roll(rows, 32 * k, 1)
        packed = jnp.where(lane48 == k, rows, packed)
    ppack[...] = packed
    for vv in range(16):
        psend[vv, 0:12, :] = pmain[12 * vv : 12 * vv + 12, :]
        psend[vv, 12:15, :] = ppack[3 * vv : 3 * vv + 3, :]
        psend[vv, 15:16, :] = jnp.zeros((1, 128), F32)
    sums = [links.start(psend.at[(v + d) % 16], precv.at[d - 1], at_v(d)) for d in range(1, 16)]

    loads["resid"].wait()
    loads["gain"].wait()
    rs[...] = jnp.zeros((16, 256), F32)
    rs[0:12, 0:160] = resid[...].astype(F32)
    gs[...] = jnp.zeros((1, 256), F32)
    gs[:, 0:160] = gain[...]
    rem[...] = jnp.zeros((16, 128), F32)

    arrived(s_zh)
    run = sg.at[c, y, x, zl]
    s_zl = [links.start(run, run, at_zl(d)) for d in range(1, 4)]

    loads["thead"].wait()
    lane = iota((192, 128), 1)

    def reorder(qq):
        last = jnp.zeros((192, 128), F32)
        off = 32 * (qq % 4)
        for h in range(4):
            first = ((h * 8 + qq) * 160) // 128
            right = thead[:, (first + 1) * 128 : (first + 2) * 128].astype(F32)
            if off == 0:
                hp[qq, h] = thead[:, first * 128 : (first + 1) * 128]
            else:
                left = thead[:, first * 128 : (first + 1) * 128].astype(F32)
                joined = jnp.where(lane < off, right, left)
                hp[qq, h] = pltpu.roll(joined, 128 - off, 1).astype(BF16)
            shift = (32 * h - off) % 128
            moved = right if shift == 0 else pltpu.roll(right, shift, 1)
            last = jnp.where(lane // 32 == h, moved, last)
        hp[qq, 4] = last.astype(BF16)

    reorder(0)
    reorder(1)

    arrived(sums)
    total = psend[v]
    for d in range(15):
        total = total + precv[d]
    for k in range(4):
        rows = total[12:15, :] if k == 0 else pltpu.roll(total, 128 - 32 * k, 1)[12:15, :]
        for j in range(3):
            rem[4 * j + k : 4 * j + k + 1, 0:32] = rows[j : j + 1, 0:32]
    pre_a = jnp.where(iota((16, 128), 0) < 12, total, 0.0) + rs[:, 0:128]
    pre_b = rem[...] + rs[:, 128:256]
    diagonal = iota((16, 128), 0) == iota((16, 128), 1)
    column = jnp.sum(pre_a * pre_a + pre_b * pre_b, axis=1, keepdims=True)
    u1[q] = jnp.sum(jnp.where(diagonal, column, 0.0), axis=0, keepdims=True)
    squares = [links.start(u1.at[q], u1.at[q], at_q(d)) for d in range(1, 8)]

    gained = pre_b * gs[:, 128:256]
    moved = gained
    for h in range(1, 4):
        moved = jnp.where(zh == h, pltpu.roll(gained, 32 * h, 1), moved)
    tz[zh, 0] = pre_a * gs[:, 0:128]
    tz[zh, 1] = moved
    t_zh = [links.start(tz.at[zh], tz.at[zh], at_zh(d)) for d in range(1, 4)]

    def spread(buf):
        one = buf.at[c, y, x, pl.ds(0, 2)]
        two = buf.at[c, y, x, pl.ds(2, 2)]
        a = [links.start(one, one, at_x(d)) for d in range(1, 4)]
        b = [links.start(two, two, at_y(d)) for d in range(1, 4)]
        return a, b

    def spread_on(buf, a, b):
        one = buf.at[c, y, :, pl.ds(0, 2)]
        two = buf.at[c, :, x, pl.ds(2, 2)]
        arrived(a)
        a = [links.start(one, one, at_y(d)) for d in range(1, 4)]
        arrived(b)
        b = [links.start(two, two, at_x(d)) for d in range(1, 4)]
        return a, b, [links.start(one, one, sibling), links.start(two, two, sibling)]

    def hand_over(buf, a, b, core):
        for d in (1, 3, 2):
            a[d - 1].wait_recv()
            one = buf.at[c, (y + 4 - d) % 4, :, pl.ds(0, 2)]
            core.append(links.start(one, one, sibling))
            b[d - 1].wait_recv()
            two = buf.at[c, :, (x + 4 - d) % 4, pl.ds(2, 2)]
            core.append(links.start(two, two, sibling))

    arrived(s_zl)
    s_a, s_b = spread(sg)
    reorder(2)
    reorder(3)

    arrived(squares)
    line = u1[0]
    for k in range(1, 8):
        line = line + u1[k]
    u2[zh] = line
    squares = [links.start(u2.at[zh], u2.at[zh], at_zh(d)) for d in range(1, 4)]
    s_a, s_b, s_core = spread_on(sg, s_a, s_b)
    reorder(4)
    reorder(5)

    arrived(squares)
    line = (u2[0] + u2[1]) + (u2[2] + u2[3])
    column = jnp.sum(jnp.where(diagonal, line, 0.0), axis=1, keepdims=True)
    scale = lax.rsqrt(column / DT + 1e-06)
    arrived(t_zh)
    for h in range(4):
        tg[c, y, x, zl, h] = (tz[h, 0] * scale).astype(BF16)
    tg[c, y, x, zl, 4] = (((tz[0, 1] + tz[1, 1]) + (tz[2, 1] + tz[3, 1])) * scale).astype(BF16)
    run = tg.at[c, y, x, zl]
    t_zl = [links.start(run, run, at_zl(d)) for d in range(1, 4)]
    reorder(6)
    reorder(7)

    loads["ids"].wait()
    loads["counts"].wait()
    line = iota((1, 256), 1)
    token = ((line // 16) % 4 * 4 + line // 64) * 12 + line % 16
    real = line % 16 < 12
    chosen = jnp.where(iota((192, 256), 0) == jnp.where(real, token, -1), 1.0, 0.0).astype(BF16)
    domain = jnp.dot(
        jnp.broadcast_to(ids[...], (8, 192)).astype(F32).astype(BF16), chosen, preferred_element_type=F32)[0:1]
    counted = jnp.zeros((1, 256), F32)
    for k in range(NDOM):
        counted = jnp.where(domain == float(k), counts[:, k : k + 1].astype(F32), counted)
    weight = TOK / NDOM / counted

    arrived(t_zl)
    t_a, t_b = spread(tg)
    hand_over(sg, s_a, s_b, s_core)

    def rows_of(buf, cc, yy, j):
        return buf[cc, yy, :, :, j].reshape(256, 128)

    def columns(cc, yy):
        return jnp.concatenate(
            [shead[:, pl.ds(pl.multiple_of((h * 8 + yy * 2 + cc) * 128, 128), 128)] for h in range(4)], axis=1)

    def student(cc, acc):
        for yy in range(4):
            right = jnp.concatenate([rows_of(sg, cc, yy, h) for h in range(4)], axis=1)
            one = lax.dot_general(columns(cc, yy), right, NT, preferred_element_type=F32)
            acc = one if acc is None else acc + one
        return acc

    def teacher(cc, acc):
        for yy in range(4):
            left = jnp.concatenate([hp[yy * 2 + cc, j] for j in range(5)], axis=1)
            right = jnp.concatenate([rows_of(tg, cc, yy, j) for j in range(5)], axis=1)
            one = lax.dot_general(left, right, NT, preferred_element_type=F32)
            acc = one if acc is None else acc + one
        return acc

    t_a, t_b, t_core = spread_on(tg, t_a, t_b)
    loads["shead"].wait()
    zs = student(c, None)
    arrived(s_core)
    zs = student(1 - c, zs)
    ms = jnp.max(zs, axis=0, keepdims=True)
    ss = jnp.sum(jnp.exp(zs - ms), axis=0, keepdims=True)
    hand_over(tg, t_a, t_b, t_core)
    zt = teacher(c, None)
    arrived(t_core)
    zt = teacher(1 - c, zt)

    mt = jnp.max(zt, axis=0, keepdims=True)
    et = jnp.exp(zt - mt)
    stats = (mt, jnp.sum(et, axis=0, keepdims=True), jnp.sum(et * (zt - zs), axis=0, keepdims=True), ms, ss)
    for buf, slot, count, peer in ((q1, v, 16, at_v), (q2, q, 8, at_q), (q3, zh, 4, at_zh)):
        own = buf.at[slot]
        for k in range(5):
            own[k] = stats[k]
        arrived([links.start(own, own, peer(d)) for d in range(1, count)])
        stats = merge(buf, count)
    mt, st, at, ms, ss = stats

    dl = jnp.exp(zs - ms) * (weight / ss) - jnp.exp(zt - mt) * (weight / st)
    dl = jnp.transpose(dl).astype(BF16)

    def blocks(cc, yy):
        return jnp.dot(dl, columns(cc, yy), preferred_element_type=F32)

    over = []
    for d in (1, 2, 3, 0):
        yy = (y + d) % 4
        piece = blocks(1 - c, yy)
        for h in range(4):
            gsend[yy, :, :, h] = piece[:, h * 128 : h * 128 + 128].astype(BF16).reshape(4, 4, 16, 128)
        over.append(links.start(gsend.at[yy], grecv.at[yy], sibling))
    r_b = []
    for k, d in enumerate((1, 2, 3, 0)):
        yy = (y + d) % 4
        piece = blocks(c, yy)
        over[k].wait_recv()
        for h in range(4):
            both = piece[:, h * 128 : h * 128 + 128].reshape(4, 4, 16, 128) + grecv[yy, :, :, h].astype(F32)
            gown[yy, :, :, h] = both
            gx[yy, :, :, h] = both.astype(BF16)
        if d > 0:
            r_b.append(links.start(gx.at[yy, :, pl.ds(2, 2)], ryb.at[d - 1], at_y(d)))
    r_a = [links.start(gx.at[:, (x + d) % 4, pl.ds(0, 2)], rxa.at[d - 1], at_x(d)) for d in range(1, 4)]

    arrived(r_b)
    acc = gown[y, :, 2:4]
    for d in range(3):
        acc = acc + ryb[d].astype(F32)
    gown[y, :, 2:4] = acc
    sb[...] = acc.astype(BF16)
    r_b = [links.start(sb.at[(x + d) % 4], rxb.at[d - 1], at_x(d)) for d in range(1, 4)]
    arrived(r_a)
    acc = gown[:, x, 0:2]
    for d in range(3):
        acc = acc + rxa[d].astype(F32)
    gown[:, x, 0:2] = acc
    sa[...] = acc.astype(BF16)
    r_a = [links.start(sa.at[(y + d) % 4], rya.at[d - 1], at_y(d)) for d in range(1, 4)]

    kl = at / st - mt - jnp.log(st) + ms + jnp.log(ss)
    loss = jnp.zeros((1, NDOM), F32)
    for k in range(NDOM):
        one = jnp.sum(jnp.where(real & (domain == float(k)), weight * kl, 0.0), axis=1, keepdims=True)
        loss = jnp.where(iota((1, NDOM), 1) == k, one, loss)
    loss_out[...] = loss

    arrived(r_b)
    acc = gown[y, x, 2:4]
    for d in range(3):
        acc = acc + rxb[d].astype(F32)
    fin[2:4] = acc
    fsend[2:4] = acc.astype(BF16)
    arrived(r_a)
    acc = gown[y, x, 0:2]
    for d in range(3):
        acc = acc + rya[d].astype(F32)
    fin[0:2] = acc
    fsend[0:2] = acc.astype(BF16)
    arrived([links.start(fsend.at[(zl + d) % 4], rzl.at[d - 1], at_zl(d)) for d in range(1, 4)])
    acc = fin[zl]
    for d in range(3):
        acc = acc + rzl[d].astype(F32)
    fin[0] = acc
    zsend[...] = acc.astype(BF16)
    arrived([links.start(zsend.at[(zh + d) % 4], rzh.at[d - 1], at_zh(d)) for d in range(1, 4)])
    acc = fin[0, zh]
    for d in range(3):
        acc = acc + rzh[d].astype(F32)
    grad_out[...] = acc[0:12, :]
    links.finish()


def per_device(t_act, t_down, t_resid, t_gain, s_hidden, t_head, s_head, domain_ids, domain_counts):
    anywhere = pl.BlockSpec(memory_space=pltpu.HBM)
    held = pl.BlockSpec(memory_space=pltpu.VMEM)

    def vmem(shape, dtype=F32):
        return pltpu.VMEM(shape, dtype)

    grad, loss = pl.pallas_call(
        body,
        out_shape=(jax.ShapeDtypeStruct((12, 128), F32), jax.ShapeDtypeStruct((1, NDOM), F32)),
        in_specs=[anywhere] * 9,
        out_specs=(held, held),
        scratch_shapes=[
            vmem((192, 1600), BF16), vmem((160, 1600), BF16), vmem((12, 160), BF16), vmem((1, 160)),
            vmem((12, 128), BF16), vmem((192, DT), BF16), vmem((192, DS), BF16), vmem((1, TOK), jnp.int32), vmem((1, NDOM), jnp.int32),
            vmem((192, 128)), vmem((192, 128)), vmem((48, 128)),
            vmem((16, 16, 128)), vmem((15, 16, 128)), vmem((16, 128)),
            vmem((16, 256)), vmem((1, 256)), vmem((8, 1, 128)), vmem((4, 1, 128)),
            vmem((8, 5, 192, 128), BF16), vmem((4, 2, 16, 128)),
            vmem((2, 4, 4, 4, 5, 16, 128), BF16), vmem((2, 4, 4, 4, 4, 16, 128), BF16),
            vmem((16, 5, 1, 256)), vmem((8, 5, 1, 256)), vmem((4, 5, 1, 256)),
            vmem((4, 4, 4, 4, 16, 128), BF16), vmem((4, 4, 4, 4, 16, 128), BF16),
            vmem((4, 4, 4, 4, 16, 128)), vmem((4, 4, 4, 4, 16, 128), BF16),
            vmem((3, 4, 2, 4, 16, 128), BF16), vmem((3, 4, 2, 4, 16, 128), BF16),
            vmem((3, 2, 4, 16, 128), BF16), vmem((3, 2, 4, 16, 128), BF16),
            vmem((4, 2, 4, 16, 128), BF16), vmem((4, 2, 4, 16, 128), BF16),
            vmem((4, 4, 16, 128)), vmem((4, 4, 16, 128), BF16), vmem((3, 4, 16, 128), BF16),
            vmem((4, 16, 128), BF16), vmem((3, 16, 128), BF16),
            pltpu.SemaphoreType.DMA((9,)), pltpu.SemaphoreType.DMA((NSEM,)), pltpu.SemaphoreType.DMA((NSEM,)),
        ],
        compiler_params=pltpu.CompilerParams(
            collective_id=0, has_side_effects=True, vmem_limit_bytes=62 * 1024 * 1024),
    )(
        t_act, t_down.T, t_resid, t_gain.reshape(1, -1), s_hidden, t_head, s_head, domain_ids.reshape(1, -1),
        domain_counts.reshape(1, -1),
    )
    return grad, loss.reshape(NDOM)


def solution(mesh):
    return jax.shard_map(
        per_device,
        mesh=mesh,
        in_specs=(
            P(None, "vocab"),
            P("vocab", "grp"),
            P("vocab", "grp"),
            P("grp"),
            P("vocab", "grp"),
            P(("grp", "vocab"), None),
            P(("grp", "vocab"), None),
            P(),
            P(),
        ),
        out_specs=(P("vocab", "grp"), P()),
        check_vma=False,
    )
```

time: 118 us -> 103 us (0.87)
  Pallas kernels: 107 us -> 99.3 us
  local copies, waits for them, and re-layouts: 9.87 us -> 2.43 us
    pallas_call x1, Pallas kernels: 107 us -> 99.3 us  [per_device(): pl.pallas_call(body, out_shape=(jax.ShapeDtypeStruct((12, 128), F32), jax...]
    unnamed x19 -> x2, local copies, waits for them, and re-layouts: 9.87 us -> 2.43 us
where the time goes in v2:
time: 103 us; the launch traced here: 102 us
  Pallas kernels  99.3 us (96%)
  local copies, waits for them, and re-layouts  2.43 us (2%)
    pallas_call x1, Pallas kernels, per_device(): pl.pallas_call(body, out_shape=(jax.ShapeDtypeStruct((12, 128), F32), jax...  99.3 us
    unnamed x2, local copies, waits for them, and re-layouts  2.43 us

profile of v2, /device:TPU:1, one launch (start us, length us, event | category | flops | bytes accessed | tf_op | source)
XLA Modules:
  0.0 102.3 jit_solution(10018946200154896939)
XLA Ops:
  0.6 99.3 %shard_map.104 = (f32[12,128]{1,0:T(8,128)}, f32[1,8]{1,0:T(1,128)}) custom-call(bf16[192,1600]{1,0:T(8,128)(2,1)} %act_hbm.1, bf16[160,1600]{1,0:T(8,128)(2,1)} %bitcast.5, bf16[12,160]{1,0:T(8,128)(2,1)} %resid_hbm.1, f32[1,160]{1,0:T(1,128)} %bitcast.6, bf16[12,128]{1,0:T(8,128)(2,1)} %hid_hbm.1, bf16[192,5120]{1,0:T(8,128)(2,1)} %thead_hbm.1, ...), custom_call_target="tpu_custom_call" | custom-call | tf_op jit(solution)/shard_map/pallas_call | solution.py:392
  99.9 1.3 %copy.13 = f32[12,128]{1,0:T(8,128)} copy(f32[12,128]{1,0:T(8,128)} %get-tuple-element.8) | data formatting | bytes 12288
  101.2 1.1 %copy.14 = f32[8]{0:T(128)} copy(f32[8]{0:T(128)} %bitcast.9) | data formatting | bytes 64

commit v3 on v2

--- a/solution.py
+++ b/solution.py
@@ -12,7 +12,7 @@
 F32 = jnp.float32
 BF16 = jnp.bfloat16
 MESH = pl.DeviceIdType.MESH
-NSEM = 160
+NSEM = 192
 NT = (((1,), (1,)), ((), ()))
 
 
@@ -38,6 +38,7 @@
     def finish(self):
         for copy in self.all:
             copy.wait_send()
+        self.all = []
 
 
 def arrived(copies):
@@ -49,7 +50,7 @@
     mt, ms = buf[0, 0], buf[0, 3]
     for k in range(1, count):
         mt, ms = jnp.maximum(mt, buf[k, 0]), jnp.maximum(ms, buf[k, 3])
-    st = at = ss = jnp.zeros((1, 256), F32)
+    st = at = ss = jnp.zeros((1, TOK), F32)
     for k in range(count):
         ft, fs = jnp.exp(buf[k, 0] - mt), jnp.exp(buf[k, 3] - ms)
         st, at, ss = st + buf[k, 1] * ft, at + buf[k, 2] * ft, ss + buf[k, 4] * fs
@@ -60,9 +61,9 @@
     act_hbm, down_hbm, resid_hbm, gain_hbm, hid_hbm, thead_hbm, shead_hbm, ids_hbm, counts_hbm,
     grad_out, loss_out,
     act, down, resid, gain, hid, thead, shead, ids, counts,
-    pmain, prem, ppack, psend, precv, rem, rs, gs, u1, u2,
-    hp, tz, tg, sg, q1, q2, q3,
-    gsend, grecv, gown, gx, rxa, ryb, rya, rxb, sa, sb, fin, fsend, rzl, zsend, rzh,
+    pmain, prem, ppack, psend, precv, rem, rs, gs, u1,
+    hp, tz, tl, tg, sl, sg, rows48, q1, q2,
+    gsend, grecv, gown, gx, rxa, ryb, rya, rxb, sa, sb, fin, zown, zsend, rz,
     load_sem, send_sem, recv_sem,
 ):
     g, v = lax.axis_index("grp"), lax.axis_index("vocab")
@@ -85,8 +86,11 @@
     def at_v(d):
         return (g, (v + d) % 16)
 
-    def at_q(d):
-        return (zh * 8 + (q + d) % 8, v)
+    def at_g(d):
+        return ((g + d) % 32, v)
+
+    def at_z(a, b):
+        return (((zh + a) % 4) * 8 + q, ((zl + b) % 4) * 4 + x)
 
     sibling = (zh * 8 + y * 2 + (1 - c), v)
 
@@ -102,19 +106,20 @@
     barrier = pltpu.get_barrier_semaphore()
     for d in range(1, 16):
         pl.semaphore_signal(barrier, inc=1, device_id=at_v(d), device_id_type=MESH)
-    for d in range(1, 8):
-        pl.semaphore_signal(barrier, inc=1, device_id=at_q(d), device_id_type=MESH)
-    for d in range(1, 4):
-        pl.semaphore_signal(barrier, inc=1, device_id=at_zh(d), device_id_type=MESH)
+    for d in range(1, 32):
+        pl.semaphore_signal(barrier, inc=1, device_id=at_g(d), device_id_type=MESH)
+    for a in range(1, 4):
+        for b in range(1, 4):
+            pl.semaphore_signal(barrier, inc=1, device_id=at_z(a, b), device_id_type=MESH)
 
     links = Links(send_sem, recv_sem)
 
     loads["hid"].wait()
-    mine = sg.at[c, y, x, zl, zh]
+    mine = sl.at[zl, zh]
     mine[...] = jnp.zeros((16, 128), BF16)
     mine[0:12, :] = hid[...]
 
-    pl.semaphore_wait(barrier, 25)
+    pl.semaphore_wait(barrier, 55)
     s_zh = [links.start(mine, mine, at_zh(d)) for d in range(1, 4)]
 
     loads["act"].wait()
@@ -142,9 +147,11 @@
     gs[...] = jnp.zeros((1, 256), F32)
     gs[:, 0:160] = gain[...]
     rem[...] = jnp.zeros((16, 128), F32)
+    zsend[...] = jnp.zeros((16, 16, 128), BF16)
+    zown[...] = jnp.zeros((16, 16, 128), F32)
 
     arrived(s_zh)
-    run = sg.at[c, y, x, zl]
+    run = sl.at[zl]
     s_zl = [links.start(run, run, at_zl(d)) for d in range(1, 4)]
 
     loads["thead"].wait()
@@ -182,8 +189,8 @@
     pre_b = rem[...] + rs[:, 128:256]
     diagonal = iota((16, 128), 0) == iota((16, 128), 1)
     column = jnp.sum(pre_a * pre_a + pre_b * pre_b, axis=1, keepdims=True)
-    u1[q] = jnp.sum(jnp.where(diagonal, column, 0.0), axis=0, keepdims=True)
-    squares = [links.start(u1.at[q], u1.at[q], at_q(d)) for d in range(1, 8)]
+    u1[g] = jnp.sum(jnp.where(diagonal, column, 0.0), axis=0, keepdims=True)
+    squares = [links.start(u1.at[g], u1.at[g], at_g(d)) for d in range(1, 32)]
 
     gained = pre_b * gs[:, 128:256]
     moved = gained
@@ -193,78 +200,89 @@
     tz[zh, 1] = moved
     t_zh = [links.start(tz.at[zh], tz.at[zh], at_zh(d)) for d in range(1, 4)]
 
-    def spread(buf):
-        one = buf.at[c, y, x, pl.ds(0, 2)]
-        two = buf.at[c, y, x, pl.ds(2, 2)]
+    def pack(src, dst, tiles):
+        for j in range(tiles):
+            for k in range(4):
+                rows48[j, 12 * k : 12 * k + 12, :] = src[k, j].astype(F32)[0:12, :]
+        for j in range(tiles):
+            dst[c, y, x, 3 * j : 3 * j + 3] = rows48[j].astype(BF16).reshape(3, 16, 128)
+
+    def cut(tiles):
+        half = (3 * tiles + 1) // 2
+        return pl.ds(0, half), pl.ds(half, 3 * tiles - half)
+
+    def spread(buf, tiles):
+        lo, hi = cut(tiles)
+        one, two = buf.at[c, y, x, lo], buf.at[c, y, x, hi]
         a = [links.start(one, one, at_x(d)) for d in range(1, 4)]
         b = [links.start(two, two, at_y(d)) for d in range(1, 4)]
         return a, b
 
-    def spread_on(buf, a, b):
-        one = buf.at[c, y, :, pl.ds(0, 2)]
-        two = buf.at[c, :, x, pl.ds(2, 2)]
+    def spread_on(buf, tiles, a, b):
+        lo, hi = cut(tiles)
+        one, two = buf.at[c, y, :, lo], buf.at[c, :, x, hi]
         arrived(a)
         a = [links.start(one, one, at_y(d)) for d in range(1, 4)]
         arrived(b)
         b = [links.start(two, two, at_x(d)) for d in range(1, 4)]
         return a, b, [links.start(one, one, sibling), links.start(two, two, sibling)]
 
-    def hand_over(buf, a, b, core):
+    def hand_over(buf, tiles, a, b, core):
+        lo, hi = cut(tiles)
         for d in (1, 3, 2):
             a[d - 1].wait_recv()
-            one = buf.at[c, (y + 4 - d) % 4, :, pl.ds(0, 2)]
+            one = buf.at[c, (y + 4 - d) % 4, :, lo]
             core.append(links.start(one, one, sibling))
             b[d - 1].wait_recv()
-            two = buf.at[c, :, (x + 4 - d) % 4, pl.ds(2, 2)]
+            two = buf.at[c, :, (x + 4 - d) % 4, hi]
             core.append(links.start(two, two, sibling))
 
     arrived(s_zl)
-    s_a, s_b = spread(sg)
+    pack(sl, sg, 4)
+    s_a, s_b = spread(sg, 4)
     reorder(2)
     reorder(3)
 
     arrived(squares)
     line = u1[0]
-    for k in range(1, 8):
+    for k in range(1, 32):
         line = line + u1[k]
-    u2[zh] = line
-    squares = [links.start(u2.at[zh], u2.at[zh], at_zh(d)) for d in range(1, 4)]
-    s_a, s_b, s_core = spread_on(sg, s_a, s_b)
-    reorder(4)
-    reorder(5)
-
-    arrived(squares)
-    line = (u2[0] + u2[1]) + (u2[2] + u2[3])
     column = jnp.sum(jnp.where(diagonal, line, 0.0), axis=1, keepdims=True)
     scale = lax.rsqrt(column / DT + 1e-06)
     arrived(t_zh)
     for h in range(4):
-        tg[c, y, x, zl, h] = (tz[h, 0] * scale).astype(BF16)
-    tg[c, y, x, zl, 4] = (((tz[0, 1] + tz[1, 1]) + (tz[2, 1] + tz[3, 1])) * scale).astype(BF16)
-    run = tg.at[c, y, x, zl]
+        tl[zl, h] = (tz[h, 0] * scale).astype(BF16)
+    tl[zl, 4] = (((tz[0, 1] + tz[1, 1]) + (tz[2, 1] + tz[3, 1])) * scale).astype(BF16)
+    run = tl.at[zl]
     t_zl = [links.start(run, run, at_zl(d)) for d in range(1, 4)]
+    s_a, s_b, s_core = spread_on(sg, 4, s_a, s_b)
+    reorder(4)
+    reorder(5)
     reorder(6)
-    reorder(7)
 
     loads["ids"].wait()
     loads["counts"].wait()
-    line = iota((1, 256), 1)
-    token = ((line // 16) % 4 * 4 + line // 64) * 12 + line % 16
-    real = line % 16 < 12
-    chosen = jnp.where(iota((192, 256), 0) == jnp.where(real, token, -1), 1.0, 0.0).astype(BF16)
+    line = iota((1, TOK), 1)
+    at = sum((line >= 48 * k).astype(jnp.int32) for k in range(1, 4))
+    line = line - 48 * at
+    run = sum((line >= 12 * k).astype(jnp.int32) for k in range(1, 4))
+    token = run * 48 + at * 12 + line - 12 * run
+    chosen = jnp.where(iota((TOK, TOK), 0) == token, 1.0, 0.0).astype(BF16)
     domain = jnp.dot(
-        jnp.broadcast_to(ids[...], (8, 192)).astype(F32).astype(BF16), chosen, preferred_element_type=F32)[0:1]
-    counted = jnp.zeros((1, 256), F32)
+        jnp.broadcast_to(ids[...], (8, TOK)).astype(F32).astype(BF16), chosen, preferred_element_type=F32)[0:1]
+    counted = jnp.zeros((1, TOK), F32)
     for k in range(NDOM):
         counted = jnp.where(domain == float(k), counts[:, k : k + 1].astype(F32), counted)
     weight = TOK / NDOM / counted
 
     arrived(t_zl)
-    t_a, t_b = spread(tg)
-    hand_over(sg, s_a, s_b, s_core)
+    pack(tl, tg, 5)
+    t_a, t_b = spread(tg, 5)
+    reorder(7)
+    hand_over(sg, 4, s_a, s_b, s_core)
 
     def rows_of(buf, cc, yy, j):
-        return buf[cc, yy, :, :, j].reshape(256, 128)
+        return buf[cc, yy, :, 3 * j : 3 * j + 3].reshape(TOK, 128)
 
     def columns(cc, yy):
         return jnp.concatenate(
@@ -285,14 +303,14 @@
             acc = one if acc is None else acc + one
         return acc
 
-    t_a, t_b, t_core = spread_on(tg, t_a, t_b)
+    t_a, t_b, t_core = spread_on(tg, 5, t_a, t_b)
     loads["shead"].wait()
     zs = student(c, None)
     arrived(s_core)
     zs = student(1 - c, zs)
     ms = jnp.max(zs, axis=0, keepdims=True)
     ss = jnp.sum(jnp.exp(zs - ms), axis=0, keepdims=True)
-    hand_over(tg, t_a, t_b, t_core)
+    hand_over(tg, 5, t_a, t_b, t_core)
     zt = teacher(c, None)
     arrived(t_core)
     zt = teacher(1 - c, zt)
@@ -300,7 +318,7 @@
     mt = jnp.max(zt, axis=0, keepdims=True)
     et = jnp.exp(zt - mt)
     stats = (mt, jnp.sum(et, axis=0, keepdims=True), jnp.sum(et * (zt - zs), axis=0, keepdims=True), ms, ss)
-    for buf, slot, count, peer in ((q1, v, 16, at_v), (q2, q, 8, at_q), (q3, zh, 4, at_zh)):
+    for buf, slot, count, peer in ((q1, v, 16, at_v), (q2, g, 32, at_g)):
         own = buf.at[slot]
         for k in range(5):
             own[k] = stats[k]
@@ -319,7 +337,7 @@
         yy = (y + d) % 4
         piece = blocks(1 - c, yy)
         for h in range(4):
-            gsend[yy, :, :, h] = piece[:, h * 128 : h * 128 + 128].astype(BF16).reshape(4, 4, 16, 128)
+            gsend[yy, :, 3 * h : 3 * h + 3] = piece[:, h * 128 : h * 128 + 128].astype(BF16).reshape(4, 3, 16, 128)
         over.append(links.start(gsend.at[yy], grecv.at[yy], sibling))
     r_b = []
     for k, d in enumerate((1, 2, 3, 0)):
@@ -327,59 +345,64 @@
         piece = blocks(c, yy)
         over[k].wait_recv()
         for h in range(4):
-            both = piece[:, h * 128 : h * 128 + 128].reshape(4, 4, 16, 128) + grecv[yy, :, :, h].astype(F32)
-            gown[yy, :, :, h] = both
-            gx[yy, :, :, h] = both.astype(BF16)
+            part = pl.ds(3 * h, 3)
+            both = piece[:, h * 128 : h * 128 + 128].reshape(4, 3, 16, 128) + grecv[yy, :, part].astype(F32)
+            gown[yy, :, part] = both
+            gx[yy, :, part] = both.astype(BF16)
         if d > 0:
-            r_b.append(links.start(gx.at[yy, :, pl.ds(2, 2)], ryb.at[d - 1], at_y(d)))
-    r_a = [links.start(gx.at[:, (x + d) % 4, pl.ds(0, 2)], rxa.at[d - 1], at_x(d)) for d in range(1, 4)]
+            r_b.append(links.start(gx.at[yy, :, pl.ds(6, 6)], ryb.at[d - 1], at_y(d)))
+    r_a = [links.start(gx.at[:, (x + d) % 4, pl.ds(0, 6)], rxa.at[d - 1], at_x(d)) for d in range(1, 4)]
 
     arrived(r_b)
-    acc = gown[y, :, 2:4]
+    acc = gown[y, :, 6:12]
     for d in range(3):
         acc = acc + ryb[d].astype(F32)
-    gown[y, :, 2:4] = acc
+    gown[y, :, 6:12] = acc
     sb[...] = acc.astype(BF16)
     r_b = [links.start(sb.at[(x + d) % 4], rxb.at[d - 1], at_x(d)) for d in range(1, 4)]
     arrived(r_a)
-    acc = gown[:, x, 0:2]
+    acc = gown[:, x, 0:6]
     for d in range(3):
         acc = acc + rxa[d].astype(F32)
-    gown[:, x, 0:2] = acc
+    gown[:, x, 0:6] = acc
     sa[...] = acc.astype(BF16)
     r_a = [links.start(sa.at[(y + d) % 4], rya.at[d - 1], at_y(d)) for d in range(1, 4)]
 
     kl = at / st - mt - jnp.log(st) + ms + jnp.log(ss)
     loss = jnp.zeros((1, NDOM), F32)
     for k in range(NDOM):
-        one = jnp.sum(jnp.where(real & (domain == float(k)), weight * kl, 0.0), axis=1, keepdims=True)
+        one = jnp.sum(jnp.where(domain == float(k), weight * kl, 0.0), axis=1, keepdims=True)
         loss = jnp.where(iota((1, NDOM), 1) == k, one, loss)
     loss_out[...] = loss
 
     arrived(r_b)
-    acc = gown[y, x, 2:4]
+    acc = gown[y, x, 6:12]
     for d in range(3):
         acc = acc + rxb[d].astype(F32)
-    fin[2:4] = acc
-    fsend[2:4] = acc.astype(BF16)
+    fin[2:4] = acc.reshape(2, 48, 128)
     arrived(r_a)
-    acc = gown[y, x, 0:2]
+    acc = gown[y, x, 0:6]
     for d in range(3):
         acc = acc + rya[d].astype(F32)
-    fin[0:2] = acc
-    fsend[0:2] = acc.astype(BF16)
-    arrived([links.start(fsend.at[(zl + d) % 4], rzl.at[d - 1], at_zl(d)) for d in range(1, 4)])
-    acc = fin[zl]
-    for d in range(3):
-        acc = acc + rzl[d].astype(F32)
-    fin[0] = acc
-    zsend[...] = acc.astype(BF16)
-    arrived([links.start(zsend.at[(zh + d) % 4], rzh.at[d - 1], at_zh(d)) for d in range(1, 4)])
-    acc = fin[0, zh]
-    for d in range(3):
-        acc = acc + rzh[d].astype(F32)
+    fin[0:2] = acc.reshape(2, 48, 128)
+
+    for h in range(4):
+        for k in range(4):
+            rows = fin[h, 12 * k : 12 * k + 12, :]
+            zown[4 * h + k, 0:12, :] = rows
+            zsend[4 * h + k, 0:12, :] = rows.astype(BF16)
+    last = []
+    for a in range(4):
+        for b in range(4):
+            if a + b > 0:
+                block = zsend.at[((zh + a) % 4) * 4 + (zl + b) % 4]
+                last.append(links.start(block, rz.at[4 * a + b - 1], at_z(a, b)))
+    links.finish()
+    arrived(last)
+    acc = zown[zh * 4 + zl]
+    for k in range(15):
+        acc = acc + rz[k].astype(F32)
     grad_out[...] = acc[0:12, :]
-    links.finish()
 
 
 def per_device(t_act, t_down, t_resid, t_gain, s_hidden, t_head, s_head, domain_ids, domain_counts):
@@ -399,17 +422,16 @@
             vmem((12, 128), BF16), vmem((192, DT), BF16), vmem((192, DS), BF16), vmem((1, TOK), jnp.int32), vmem((1, NDOM), jnp.int32),
             vmem((192, 128)), vmem((192, 128)), vmem((48, 128)),
             vmem((16, 16, 128)), vmem((15, 16, 128)), vmem((16, 128)),
-            vmem((16, 256)), vmem((1, 256)), vmem((8, 1, 128)), vmem((4, 1, 128)),
-            vmem((8, 5, 192, 128), BF16), vmem((4, 2, 16, 128)),
-            vmem((2, 4, 4, 4, 5, 16, 128), BF16), vmem((2, 4, 4, 4, 4, 16, 128), BF16),
-            vmem((16, 5, 1, 256)), vmem((8, 5, 1, 256)), vmem((4, 5, 1, 256)),
-            vmem((4, 4, 4, 4, 16, 128), BF16), vmem((4, 4, 4, 4, 16, 128), BF16),
-            vmem((4, 4, 4, 4, 16, 128)), vmem((4, 4, 4, 4, 16, 128), BF16),
-            vmem((3, 4, 2, 4, 16, 128), BF16), vmem((3, 4, 2, 4, 16, 128), BF16),
-            vmem((3, 2, 4, 16, 128), BF16), vmem((3, 2, 4, 16, 128), BF16),
-            vmem((4, 2, 4, 16, 128), BF16), vmem((4, 2, 4, 16, 128), BF16),
-            vmem((4, 4, 16, 128)), vmem((4, 4, 16, 128), BF16), vmem((3, 4, 16, 128), BF16),
-            vmem((4, 16, 128), BF16), vmem((3, 16, 128), BF16),
+            vmem((16, 256)), vmem((1, 256)), vmem((32, 1, 128)),
+            vmem((8, 5, 192, 128), BF16), vmem((4, 2, 16, 128)), vmem((4, 5, 16, 128), BF16),
+            vmem((2, 4, 4, 15, 16, 128), BF16), vmem((4, 4, 16, 128), BF16), vmem((2, 4, 4, 12, 16, 128), BF16),
+            vmem((5, 48, 128)), vmem((16, 5, 1, TOK)), vmem((32, 5, 1, TOK)),
+            vmem((4, 4, 12, 16, 128), BF16), vmem((4, 4, 12, 16, 128), BF16),
+            vmem((4, 4, 12, 16, 128)), vmem((4, 4, 12, 16, 128), BF16),
+            vmem((3, 4, 6, 16, 128), BF16), vmem((3, 4, 6, 16, 128), BF16),
+            vmem((3, 6, 16, 128), BF16), vmem((3, 6, 16, 128), BF16),
+            vmem((4, 6, 16, 128), BF16), vmem((4, 6, 16, 128), BF16),
+            vmem((4, 48, 128)), vmem((16, 16, 128)), vmem((16, 16, 128), BF16), vmem((15, 16, 128), BF16),
             pltpu.SemaphoreType.DMA((9,)), pltpu.SemaphoreType.DMA((NSEM,)), pltpu.SemaphoreType.DMA((NSEM,)),
         ],
         compiler_params=pltpu.CompilerParams(

time: 103 us -> 100 us (0.971)
  Pallas kernels: 99.3 us -> 96.7 us
    pallas_call x1, Pallas kernels: 99.3 us -> 96.7 us  [per_device(): pl.pallas_call(body, out_shape=(jax.ShapeDtypeStruct((12, 128), F32), jax...]
where the time goes in v3:
time: 100 us; the launch traced here: 99.8 us
  Pallas kernels  96.7 us (97%)
  local copies, waits for them, and re-layouts  2.43 us (2%)
    pallas_call x1, Pallas kernels, per_device(): pl.pallas_call(body, out_shape=(jax.ShapeDtypeStruct((12, 128), F32), jax...  96.7 us
    unnamed x2, local copies, waits for them, and re-layouts  2.43 us

profile of v3, /device:TPU:1, one launch (start us, length us, event | category | flops | bytes accessed | tf_op | source)
XLA Modules:
  0.0 99.8 jit_solution(9296508763690370249)
XLA Ops:
  0.6 96.7 %shard_map.104 = (f32[12,128]{1,0:T(8,128)}, f32[1,8]{1,0:T(1,128)}) custom-call(bf16[192,1600]{1,0:T(8,128)(2,1)} %act_hbm.1, bf16[160,1600]{1,0:T(8,128)(2,1)} %bitcast.5, bf16[12,160]{1,0:T(8,128)(2,1)} %resid_hbm.1, f32[1,160]{1,0:T(1,128)} %bitcast.6, bf16[12,128]{1,0:T(8,128)(2,1)} %hid_hbm.1, bf16[192,5120]{1,0:T(8,128)(2,1)} %thead_hbm.1, ...), custom_call_target="tpu_custom_call" | custom-call | tf_op jit(solution)/shard_map/pallas_call | solution.py:415
  97.4 1.3 %copy.13 = f32[12,128]{1,0:T(8,128)} copy(f32[12,128]{1,0:T(8,128)} %get-tuple-element.8) | data formatting | bytes 12288
  98.7 1.1 %copy.14 = f32[8]{0:T(128)} copy(f32[8]{0:T(128)} %bitcast.9) | data formatting | bytes 64

commit v4 on v3

--- a/solution.py
+++ b/solution.py
@@ -61,37 +61,26 @@
     act_hbm, down_hbm, resid_hbm, gain_hbm, hid_hbm, thead_hbm, shead_hbm, ids_hbm, counts_hbm,
     grad_out, loss_out,
     act, down, resid, gain, hid, thead, shead, ids, counts,
-    pmain, prem, ppack, psend, precv, rem, rs, gs, u1,
-    hp, tz, tl, tg, sl, sg, rows48, q1, q2,
-    gsend, grecv, gown, gx, rxa, ryb, rya, rxb, sa, sb, fin, zown, zsend, rz,
+    pmain, prem, ppack, psend, precv, rem, rs, gs, u1, u2,
+    hp, tz, tl, tg, sl, sg, rows48, q1, q2, q3,
+    gsend, grecv, gown, gx, rxa, ryb, rya, rxb, sa, sb, fin, fown, fsend, rzl, zsend, rzh,
     load_sem, send_sem, recv_sem,
 ):
     g, v = lax.axis_index("grp"), lax.axis_index("vocab")
-    zh, y, c = g // 8, (g // 2) % 4, g % 2
-    zl, x = v // 4, v % 4
-    q = g % 8
-
-    def at_x(d):
-        return (g, zl * 4 + (x + d) % 4)
-
-    def at_y(d):
-        return (zh * 8 + ((y + d) % 4) * 2 + c, v)
-
-    def at_zl(d):
-        return (g, ((zl + d) % 4) * 4 + x)
-
-    def at_zh(d):
-        return (((zh + d) % 4) * 8 + q, v)
-
-    def at_v(d):
-        return (g, (v + d) % 16)
-
-    def at_g(d):
-        return ((g + d) % 32, v)
-
-    def at_z(a, b):
-        return (((zh + a) % 4) * 8 + q, ((zl + b) % 4) * 4 + x)
-
+    zh, q = lax.div(g, 8), lax.rem(g, 8)
+    y, c = lax.div(q, 2), lax.rem(q, 2)
+    zl, x = lax.div(v, 4), lax.rem(v, 4)
+    xs = [x] + [lax.rem(x + d, 4) for d in range(1, 4)]
+    ys = [y] + [lax.rem(y + d, 4) for d in range(1, 4)]
+    zls = [zl] + [lax.rem(zl + d, 4) for d in range(1, 4)]
+    zhs = [zh] + [lax.rem(zh + d, 4) for d in range(1, 4)]
+    vs = [v] + [lax.rem(v + d, 16) for d in range(1, 16)]
+    at_x = [(g, zl * 4 + to) for to in xs]
+    at_y = [(zh * 8 + to * 2 + c, v) for to in ys]
+    at_zl = [(g, to * 4 + x) for to in zls]
+    at_zh = [(to * 8 + q, v) for to in zhs]
+    at_v = [(g, to) for to in vs]
+    at_q = [(zh * 8 + lax.rem(q + d, 8), v) for d in range(8)]
     sibling = (zh * 8 + y * 2 + (1 - c), v)
 
     loads = {}
@@ -105,12 +94,11 @@
 
     barrier = pltpu.get_barrier_semaphore()
     for d in range(1, 16):
-        pl.semaphore_signal(barrier, inc=1, device_id=at_v(d), device_id_type=MESH)
-    for d in range(1, 32):
-        pl.semaphore_signal(barrier, inc=1, device_id=at_g(d), device_id_type=MESH)
-    for a in range(1, 4):
-        for b in range(1, 4):
-            pl.semaphore_signal(barrier, inc=1, device_id=at_z(a, b), device_id_type=MESH)
+        pl.semaphore_signal(barrier, inc=1, device_id=at_v[d], device_id_type=MESH)
+    for d in range(1, 8):
+        pl.semaphore_signal(barrier, inc=1, device_id=at_q[d], device_id_type=MESH)
+    for d in range(1, 4):
+        pl.semaphore_signal(barrier, inc=1, device_id=at_zh[d], device_id_type=MESH)
 
     links = Links(send_sem, recv_sem)
 
@@ -119,8 +107,8 @@
     mine[...] = jnp.zeros((16, 128), BF16)
     mine[0:12, :] = hid[...]
 
-    pl.semaphore_wait(barrier, 55)
-    s_zh = [links.start(mine, mine, at_zh(d)) for d in range(1, 4)]
+    pl.semaphore_wait(barrier, 25)
+    s_zh = [links.start(mine, mine, at_zh[d]) for d in range(1, 4)]
 
     loads["act"].wait()
     loads["down"].wait()
@@ -138,7 +126,7 @@
         psend[vv, 0:12, :] = pmain[12 * vv : 12 * vv + 12, :]
         psend[vv, 12:15, :] = ppack[3 * vv : 3 * vv + 3, :]
         psend[vv, 15:16, :] = jnp.zeros((1, 128), F32)
-    sums = [links.start(psend.at[(v + d) % 16], precv.at[d - 1], at_v(d)) for d in range(1, 16)]
+    sums = [links.start(psend.at[vs[d]], precv.at[d - 1], at_v[d]) for d in range(1, 16)]
 
     loads["resid"].wait()
     loads["gain"].wait()
@@ -147,35 +135,40 @@
     gs[...] = jnp.zeros((1, 256), F32)
     gs[:, 0:160] = gain[...]
     rem[...] = jnp.zeros((16, 128), F32)
-    zsend[...] = jnp.zeros((16, 16, 128), BF16)
-    zown[...] = jnp.zeros((16, 16, 128), F32)
+    fsend[...] = jnp.zeros((4, 4, 16, 128), BF16)
+    fown[...] = jnp.zeros((4, 4, 16, 128), F32)
 
     arrived(s_zh)
     run = sl.at[zl]
-    s_zl = [links.start(run, run, at_zl(d)) for d in range(1, 4)]
+    s_zl = [links.start(run, run, at_zl[d]) for d in range(1, 4)]
 
     loads["thead"].wait()
-    lane = iota((192, 128), 1)
-
-    def reorder(qq):
-        last = jnp.zeros((192, 128), F32)
-        off = 32 * (qq % 4)
-        for h in range(4):
-            first = ((h * 8 + qq) * 160) // 128
-            right = thead[:, (first + 1) * 128 : (first + 2) * 128].astype(F32)
-            if off == 0:
-                hp[qq, h] = thead[:, first * 128 : (first + 1) * 128]
-            else:
-                left = thead[:, first * 128 : (first + 1) * 128].astype(F32)
-                joined = jnp.where(lane < off, right, left)
-                hp[qq, h] = pltpu.roll(joined, 128 - off, 1).astype(BF16)
-            shift = (32 * h - off) % 128
-            moved = right if shift == 0 else pltpu.roll(right, shift, 1)
-            last = jnp.where(lane // 32 == h, moved, last)
-        hp[qq, 4] = last.astype(BF16)
+    lane = iota((16, 128), 1)
+
+    def reorder(third):
+        def rows16(step, carry):
+            rows = pl.ds(pl.multiple_of(third * 64 + step * 16, 16), 16)
+            for qq in range(8):
+                last = jnp.zeros((16, 128), F32)
+                off = 32 * (qq % 4)
+                for h in range(4):
+                    first = ((h * 8 + qq) * 160) // 128
+                    right = thead[rows, (first + 1) * 128 : (first + 2) * 128].astype(F32)
+                    if off == 0:
+                        hp[qq, h, rows, :] = thead[rows, first * 128 : (first + 1) * 128]
+                    else:
+                        left = thead[rows, first * 128 : (first + 1) * 128].astype(F32)
+                        joined = jnp.where(lane < off, right, left)
+                        hp[qq, h, rows, :] = pltpu.roll(joined, 128 - off, 1).astype(BF16)
+                    shift = (32 * h - off) % 128
+                    moved = right if shift == 0 else pltpu.roll(right, shift, 1)
+                    last = jnp.where(lane // 32 == h, moved, last)
+                hp[qq, 4, rows, :] = last.astype(BF16)
+            return carry
+
+        lax.fori_loop(0, 4, rows16, 0)
 
     reorder(0)
-    reorder(1)
 
     arrived(sums)
     total = psend[v]
@@ -189,8 +182,8 @@
     pre_b = rem[...] + rs[:, 128:256]
     diagonal = iota((16, 128), 0) == iota((16, 128), 1)
     column = jnp.sum(pre_a * pre_a + pre_b * pre_b, axis=1, keepdims=True)
-    u1[g] = jnp.sum(jnp.where(diagonal, column, 0.0), axis=0, keepdims=True)
-    squares = [links.start(u1.at[g], u1.at[g], at_g(d)) for d in range(1, 32)]
+    u1[q] = jnp.sum(jnp.where(diagonal, column, 0.0), axis=0, keepdims=True)
+    squares = [links.start(u1.at[q], u1.at[q], at_q[d]) for d in range(1, 8)]
 
     gained = pre_b * gs[:, 128:256]
     moved = gained
@@ -198,7 +191,7 @@
         moved = jnp.where(zh == h, pltpu.roll(gained, 32 * h, 1), moved)
     tz[zh, 0] = pre_a * gs[:, 0:128]
     tz[zh, 1] = moved
-    t_zh = [links.start(tz.at[zh], tz.at[zh], at_zh(d)) for d in range(1, 4)]
+    t_zh = [links.start(tz.at[zh], tz.at[zh], at_zh[d]) for d in range(1, 4)]
 
     def pack(src, dst, tiles):
         for j in range(tiles):
@@ -214,39 +207,44 @@
     def spread(buf, tiles):
         lo, hi = cut(tiles)
         one, two = buf.at[c, y, x, lo], buf.at[c, y, x, hi]
-        a = [links.start(one, one, at_x(d)) for d in range(1, 4)]
-        b = [links.start(two, two, at_y(d)) for d in range(1, 4)]
+        a = [links.start(one, one, at_x[d]) for d in range(1, 4)]
+        b = [links.start(two, two, at_y[d]) for d in range(1, 4)]
         return a, b
 
     def spread_on(buf, tiles, a, b):
         lo, hi = cut(tiles)
         one, two = buf.at[c, y, :, lo], buf.at[c, :, x, hi]
         arrived(a)
-        a = [links.start(one, one, at_y(d)) for d in range(1, 4)]
+        a = [links.start(one, one, at_y[d]) for d in range(1, 4)]
         arrived(b)
-        b = [links.start(two, two, at_x(d)) for d in range(1, 4)]
+        b = [links.start(two, two, at_x[d]) for d in range(1, 4)]
         return a, b, [links.start(one, one, sibling), links.start(two, two, sibling)]
 
     def hand_over(buf, tiles, a, b, core):
         lo, hi = cut(tiles)
         for d in (1, 3, 2):
             a[d - 1].wait_recv()
-            one = buf.at[c, (y + 4 - d) % 4, :, lo]
+            one = buf.at[c, ys[4 - d], :, lo]
             core.append(links.start(one, one, sibling))
             b[d - 1].wait_recv()
-            two = buf.at[c, :, (x + 4 - d) % 4, hi]
+            two = buf.at[c, :, xs[4 - d], hi]
             core.append(links.start(two, two, sibling))
 
     arrived(s_zl)
     pack(sl, sg, 4)
     s_a, s_b = spread(sg, 4)
-    reorder(2)
-    reorder(3)
 
     arrived(squares)
     line = u1[0]
-    for k in range(1, 32):
+    for k in range(1, 8):
         line = line + u1[k]
+    u2[zh] = line
+    squares = [links.start(u2.at[zh], u2.at[zh], at_zh[d]) for d in range(1, 4)]
+    s_a, s_b, s_core = spread_on(sg, 4, s_a, s_b)
+    reorder(1)
+
+    arrived(squares)
+    line = (u2[0] + u2[1]) + (u2[2] + u2[3])
     column = jnp.sum(jnp.where(diagonal, line, 0.0), axis=1, keepdims=True)
     scale = lax.rsqrt(column / DT + 1e-06)
     arrived(t_zh)
@@ -254,11 +252,8 @@
         tl[zl, h] = (tz[h, 0] * scale).astype(BF16)
     tl[zl, 4] = (((tz[0, 1] + tz[1, 1]) + (tz[2, 1] + tz[3, 1])) * scale).astype(BF16)
     run = tl.at[zl]
-    t_zl = [links.start(run, run, at_zl(d)) for d in range(1, 4)]
-    s_a, s_b, s_core = spread_on(sg, 4, s_a, s_b)
-    reorder(4)
-    reorder(5)
-    reorder(6)
+    t_zl = [links.start(run, run, at_zl[d]) for d in range(1, 4)]
+    reorder(2)
 
     loads["ids"].wait()
     loads["counts"].wait()
@@ -278,7 +273,6 @@
     arrived(t_zl)
     pack(tl, tg, 5)
     t_a, t_b = spread(tg, 5)
-    reorder(7)
     hand_over(sg, 4, s_a, s_b, s_core)
 
     def rows_of(buf, cc, yy, j):
@@ -318,11 +312,11 @@
     mt = jnp.max(zt, axis=0, keepdims=True)
     et = jnp.exp(zt - mt)
     stats = (mt, jnp.sum(et, axis=0, keepdims=True), jnp.sum(et * (zt - zs), axis=0, keepdims=True), ms, ss)
-    for buf, slot, count, peer in ((q1, v, 16, at_v), (q2, g, 32, at_g)):
+    for buf, slot, count, peer in ((q1, v, 16, at_v), (q2, q, 8, at_q), (q3, zh, 4, at_zh)):
         own = buf.at[slot]
         for k in range(5):
             own[k] = stats[k]
-        arrived([links.start(own, own, peer(d)) for d in range(1, count)])
+        arrived([links.start(own, own, peer[d]) for d in range(1, count)])
         stats = merge(buf, count)
     mt, st, at, ms, ss = stats
 
@@ -334,14 +328,14 @@
 
     over = []
     for d in (1, 2, 3, 0):
-        yy = (y + d) % 4
+        yy = ys[d]
         piece = blocks(1 - c, yy)
         for h in range(4):
             gsend[yy, :, 3 * h : 3 * h + 3] = piece[:, h * 128 : h * 128 + 128].astype(BF16).reshape(4, 3, 16, 128)
         over.append(links.start(gsend.at[yy], grecv.at[yy], sibling))
     r_b = []
     for k, d in enumerate((1, 2, 3, 0)):
-        yy = (y + d) % 4
+        yy = ys[d]
         piece = blocks(c, yy)
         over[k].wait_recv()
         for h in range(4):
@@ -350,8 +344,8 @@
             gown[yy, :, part] = both
             gx[yy, :, part] = both.astype(BF16)
         if d > 0:
-            r_b.append(links.start(gx.at[yy, :, pl.ds(6, 6)], ryb.at[d - 1], at_y(d)))
-    r_a = [links.start(gx.at[:, (x + d) % 4, pl.ds(0, 6)], rxa.at[d - 1], at_x(d)) for d in range(1, 4)]
+            r_b.append(links.start(gx.at[yy, :, pl.ds(6, 6)], ryb.at[d - 1], at_y[d]))
+    r_a = [links.start(gx.at[:, xs[d], pl.ds(0, 6)], rxa.at[d - 1], at_x[d]) for d in range(1, 4)]
 
     arrived(r_b)
     acc = gown[y, :, 6:12]
@@ -359,14 +353,14 @@
         acc = acc + ryb[d].astype(F32)
     gown[y, :, 6:12] = acc
     sb[...] = acc.astype(BF16)
-    r_b = [links.start(sb.at[(x + d) % 4], rxb.at[d - 1], at_x(d)) for d in range(1, 4)]
+    r_b = [links.start(sb.at[xs[d]], rxb.at[d - 1], at_x[d]) for d in range(1, 4)]
     arrived(r_a)
     acc = gown[:, x, 0:6]
     for d in range(3):
         acc = acc + rxa[d].astype(F32)
     gown[:, x, 0:6] = acc
     sa[...] = acc.astype(BF16)
-    r_a = [links.start(sa.at[(y + d) % 4], rya.at[d - 1], at_y(d)) for d in range(1, 4)]
+    r_a = [links.start(sa.at[ys[d]], rya.at[d - 1], at_y[d]) for d in range(1, 4)]
 
     kl = at / st - mt - jnp.log(st) + ms + jnp.log(ss)
     loss = jnp.zeros((1, NDOM), F32)
@@ -389,20 +383,22 @@
     for h in range(4):
         for k in range(4):
             rows = fin[h, 12 * k : 12 * k + 12, :]
-            zown[4 * h + k, 0:12, :] = rows
-            zsend[4 * h + k, 0:12, :] = rows.astype(BF16)
-    last = []
-    for a in range(4):
-        for b in range(4):
-            if a + b > 0:
-                block = zsend.at[((zh + a) % 4) * 4 + (zl + b) % 4]
-                last.append(links.start(block, rz.at[4 * a + b - 1], at_z(a, b)))
+            fown[k, h, 0:12, :] = rows
+            fsend[k, h, 0:12, :] = rows.astype(BF16)
+    last = [links.start(fsend.at[zls[d]], rzl.at[d - 1], at_zl[d]) for d in range(1, 4)]
     links.finish()
     arrived(last)
-    acc = zown[zh * 4 + zl]
-    for k in range(15):
-        acc = acc + rz[k].astype(F32)
+    acc = fown[zl]
+    for d in range(3):
+        acc = acc + rzl[d].astype(F32)
+    fown[0] = acc
+    zsend[...] = acc.astype(BF16)
+    arrived([links.start(zsend.at[zhs[d]], rzh.at[d - 1], at_zh[d]) for d in range(1, 4)])
+    acc = fown[0, zh]
+    for d in range(3):
+        acc = acc + rzh[d].astype(F32)
     grad_out[...] = acc[0:12, :]
+    links.finish()
 
 
 def per_device(t_act, t_down, t_resid, t_gain, s_hidden, t_head, s_head, domain_ids, domain_counts):
@@ -422,16 +418,17 @@
             vmem((12, 128), BF16), vmem((192, DT), BF16), vmem((192, DS), BF16), vmem((1, TOK), jnp.int32), vmem((1, NDOM), jnp.int32),
             vmem((192, 128)), vmem((192, 128)), vmem((48, 128)),
             vmem((16, 16, 128)), vmem((15, 16, 128)), vmem((16, 128)),
-            vmem((16, 256)), vmem((1, 256)), vmem((32, 1, 128)),
+            vmem((16, 256)), vmem((1, 256)), vmem((8, 1, 128)), vmem((4, 1, 128)),
             vmem((8, 5, 192, 128), BF16), vmem((4, 2, 16, 128)), vmem((4, 5, 16, 128), BF16),
             vmem((2, 4, 4, 15, 16, 128), BF16), vmem((4, 4, 16, 128), BF16), vmem((2, 4, 4, 12, 16, 128), BF16),
-            vmem((5, 48, 128)), vmem((16, 5, 1, TOK)), vmem((32, 5, 1, TOK)),
+            vmem((5, 48, 128)), vmem((16, 5, 1, TOK)), vmem((8, 5, 1, TOK)), vmem((4, 5, 1, TOK)),
             vmem((4, 4, 12, 16, 128), BF16), vmem((4, 4, 12, 16, 128), BF16),
             vmem((4, 4, 12, 16, 128)), vmem((4, 4, 12, 16, 128), BF16),
             vmem((3, 4, 6, 16, 128), BF16), vmem((3, 4, 6, 16, 128), BF16),
             vmem((3, 6, 16, 128), BF16), vmem((3, 6, 16, 128), BF16),
             vmem((4, 6, 16, 128), BF16), vmem((4, 6, 16, 128), BF16),
-            vmem((4, 48, 128)), vmem((16, 16, 128)), vmem((16, 16, 128), BF16), vmem((15, 16, 128), BF16),
+            vmem((4, 48, 128)), vmem((4, 4, 16, 128)), vmem((4, 4, 16, 128), BF16), vmem((3, 4, 16, 128), BF16),
+            vmem((4, 16, 128), BF16), vmem((3, 16, 128), BF16),
             pltpu.SemaphoreType.DMA((9,)), pltpu.SemaphoreType.DMA((NSEM,)), pltpu.SemaphoreType.DMA((NSEM,)),
         ],
         compiler_params=pltpu.CompilerParams(

time: 100 us -> 99.6 us (level)
  no operation moved by 1% of the time
where the time goes in v4:
time: 99.6 us; the launch traced here: 99 us
  Pallas kernels  95.9 us (96%)
  local copies, waits for them, and re-layouts  2.43 us (2%)
    pallas_call x1, Pallas kernels, per_device(): pl.pallas_call(body, out_shape=(jax.ShapeDtypeStruct((12, 128), F32), jax...  95.9 us
    unnamed x2, local copies, waits for them, and re-layouts  2.43 us

profile of v4, /device:TPU:1, one launch (start us, length us, event | category | flops | bytes accessed | tf_op | source)
XLA Modules:
  0.0 99.0 jit_solution(14591261176167330510)
XLA Ops:
  0.6 95.9 %shard_map.104 = (f32[12,128]{1,0:T(8,128)}, f32[1,8]{1,0:T(1,128)}) custom-call(bf16[192,1600]{1,0:T(8,128)(2,1)} %act_hbm.1, bf16[160,1600]{1,0:T(8,128)(2,1)} %bitcast.5, bf16[12,160]{1,0:T(8,128)(2,1)} %resid_hbm.1, f32[1,160]{1,0:T(1,128)} %bitcast.6, bf16[12,128]{1,0:T(8,128)(2,1)} %hid_hbm.1, bf16[192,5120]{1,0:T(8,128)(2,1)} %thead_hbm.1, ...), custom_call_target="tpu_custom_call" | custom-call | tf_op jit(solution)/shard_map/pallas_call | solution.py:411
  96.6 1.3 %copy.13 = f32[12,128]{1,0:T(8,128)} copy(f32[12,128]{1,0:T(8,128)} %get-tuple-element.8) | data formatting | bytes 12288
  97.9 1.1 %copy.14 = f32[8]{0:T(128)} copy(f32[8]{0:T(128)} %bitcast.9) | data formatting | bytes 64

commit v5 on v4

--- a/solution.py
+++ b/solution.py
@@ -24,16 +24,25 @@
     def __init__(self, send, recv):
         self.send, self.recv, self.used, self.all = send, recv, 0, []
 
-    def start(self, src, dst, device):
-        k = self.used
-        self.used += 1
-        copy = pltpu.make_async_remote_copy(
+    def at(self, k, src, dst, device):
+        return pltpu.make_async_remote_copy(
             src_ref=src, dst_ref=dst, send_sem=self.send.at[k], recv_sem=self.recv.at[k],
             device_id=device, device_id_type=MESH,
         )
+
+    def start(self, src, dst, device):
+        copy = self.at(self.used, src, dst, device)
+        self.used += 1
         copy.start()
         self.all.append(copy)
         return copy
+
+    def group(self, count, describe):
+        first = self.used
+        self.used += count
+        copies = [self.at(first + k, *describe(k)) for k in range(count)]
+        self.all += copies
+        return first, copies
 
     def finish(self):
         for copy in self.all:
@@ -62,7 +71,7 @@
     grad_out, loss_out,
     act, down, resid, gain, hid, thead, shead, ids, counts,
     pmain, prem, ppack, psend, precv, rem, rs, gs, u1, u2,
-    hp, tz, tl, tg, sl, sg, rows48, q1, q2, q3,
+    hp, tz, tl, tg, sl, sg, rows48, q1, q2, q3, zs_ref, zt_ref, dl_ref,
     gsend, grecv, gown, gx, rxa, ryb, rya, rxb, sa, sb, fin, fown, fsend, rzl, zsend, rzh,
     load_sem, send_sem, recv_sem,
 ):
@@ -85,11 +94,12 @@
 
     loads = {}
     for k, (name, src, dst) in enumerate((
-        ("hid", hid_hbm, hid), ("act", act_hbm, act), ("down", down_hbm, down), ("resid", resid_hbm, resid),
-        ("gain", gain_hbm, gain), ("ids", ids_hbm, ids), ("counts", counts_hbm, counts), ("thead", thead_hbm, thead),
+        ("act", act_hbm, act), ("down", down_hbm, down), ("hid", hid_hbm, hid), ("resid", resid_hbm, resid),
+        ("gain", gain_hbm, gain), ("thead", thead_hbm, thead), ("ids", ids_hbm, ids), ("counts", counts_hbm, counts),
         ("shead", shead_hbm, shead),
     )):
         loads[name] = pltpu.make_async_copy(src, dst, load_sem.at[k])
+    for name in ("act", "down", "hid"):
         loads[name].start()
 
     barrier = pltpu.get_barrier_semaphore()
@@ -99,6 +109,9 @@
         pl.semaphore_signal(barrier, inc=1, device_id=at_q[d], device_id_type=MESH)
     for d in range(1, 4):
         pl.semaphore_signal(barrier, inc=1, device_id=at_zh[d], device_id_type=MESH)
+
+    for name in ("resid", "gain", "thead", "ids", "counts", "shead"):
+        loads[name].start()
 
     links = Links(send_sem, recv_sem)
 
@@ -135,6 +148,8 @@
     gs[...] = jnp.zeros((1, 256), F32)
     gs[:, 0:160] = gain[...]
     rem[...] = jnp.zeros((16, 128), F32)
+    zs_ref[...] = jnp.zeros((192, TOK), F32)
+    zt_ref[...] = jnp.zeros((192, TOK), F32)
     fsend[...] = jnp.zeros((4, 4, 16, 128), BF16)
     fown[...] = jnp.zeros((4, 4, 16, 128), F32)
 
@@ -282,33 +297,36 @@
         return jnp.concatenate(
             [shead[:, pl.ds(pl.multiple_of((h * 8 + yy * 2 + cc) * 128, 128), 128)] for h in range(4)], axis=1)
 
-    def student(cc, acc):
-        for yy in range(4):
+    def student(cc):
+        def one(yy, carry):
             right = jnp.concatenate([rows_of(sg, cc, yy, h) for h in range(4)], axis=1)
-            one = lax.dot_general(columns(cc, yy), right, NT, preferred_element_type=F32)
-            acc = one if acc is None else acc + one
-        return acc
-
-    def teacher(cc, acc):
-        for yy in range(4):
+            zs_ref[...] += lax.dot_general(columns(cc, yy), right, NT, preferred_element_type=F32)
+            return carry
+
+        lax.fori_loop(0, 4, one, 0)
+
+    def teacher(cc):
+        def one(yy, carry):
             left = jnp.concatenate([hp[yy * 2 + cc, j] for j in range(5)], axis=1)
             right = jnp.concatenate([rows_of(tg, cc, yy, j) for j in range(5)], axis=1)
-            one = lax.dot_general(left, right, NT, preferred_element_type=F32)
-            acc = one if acc is None else acc + one
-        return acc
+            zt_ref[...] += lax.dot_general(left, right, NT, preferred_element_type=F32)
+            return carry
+
+        lax.fori_loop(0, 4, one, 0)
 
     t_a, t_b, t_core = spread_on(tg, 5, t_a, t_b)
     loads["shead"].wait()
-    zs = student(c, None)
+    student(c)
     arrived(s_core)
-    zs = student(1 - c, zs)
+    student(1 - c)
+    zs = zs_ref[...]
     ms = jnp.max(zs, axis=0, keepdims=True)
     ss = jnp.sum(jnp.exp(zs - ms), axis=0, keepdims=True)
     hand_over(tg, 5, t_a, t_b, t_core)
-    zt = teacher(c, None)
+    teacher(c)
     arrived(t_core)
-    zt = teacher(1 - c, zt)
-
+    teacher(1 - c)
+    zs, zt = zs_ref[...], zt_ref[...]
     mt = jnp.max(zt, axis=0, keepdims=True)
     et = jnp.exp(zt - mt)
     stats = (mt, jnp.sum(et, axis=0, keepdims=True), jnp.sum(et * (zt - zs), axis=0, keepdims=True), ms, ss)
@@ -320,31 +338,49 @@
         stats = merge(buf, count)
     mt, st, at, ms, ss = stats
 
+    zs, zt = zs_ref[...], zt_ref[...]
     dl = jnp.exp(zs - ms) * (weight / ss) - jnp.exp(zt - mt) * (weight / st)
-    dl = jnp.transpose(dl).astype(BF16)
+    dl_ref[...] = jnp.transpose(dl).astype(BF16)
 
     def blocks(cc, yy):
-        return jnp.dot(dl, columns(cc, yy), preferred_element_type=F32)
-
-    over = []
-    for d in (1, 2, 3, 0):
-        yy = ys[d]
-        piece = blocks(1 - c, yy)
+        return jnp.dot(dl_ref[...], columns(cc, yy), preferred_element_type=F32)
+
+    def row(k):
+        return lax.rem(y + k + 1, 4)
+
+    def to_other(k):
+        return gsend.at[row(k)], grecv.at[row(k)], sibling
+
+    def along_y(k):
+        return gx.at[row(k), :, pl.ds(6, 6)], ryb.at[k], (zh * 8 + row(k) * 2 + c, v)
+
+    o_first, over = links.group(4, to_other)
+    b_first, r_b = links.group(3, along_y)
+
+    def give(k, carry):
+        piece = blocks(1 - c, row(k))
         for h in range(4):
-            gsend[yy, :, 3 * h : 3 * h + 3] = piece[:, h * 128 : h * 128 + 128].astype(BF16).reshape(4, 3, 16, 128)
-        over.append(links.start(gsend.at[yy], grecv.at[yy], sibling))
-    r_b = []
-    for k, d in enumerate((1, 2, 3, 0)):
-        yy = ys[d]
-        piece = blocks(c, yy)
-        over[k].wait_recv()
+            gsend[row(k), :, 3 * h : 3 * h + 3] = piece[:, h * 128 : h * 128 + 128].astype(BF16).reshape(4, 3, 16, 128)
+        links.at(o_first + k, *to_other(k)).start()
+        return carry
+
+    def keep(k, carry):
+        piece = blocks(c, row(k))
+        links.at(o_first + k, *to_other(k)).wait_recv()
         for h in range(4):
             part = pl.ds(3 * h, 3)
-            both = piece[:, h * 128 : h * 128 + 128].reshape(4, 3, 16, 128) + grecv[yy, :, part].astype(F32)
-            gown[yy, :, part] = both
-            gx[yy, :, part] = both.astype(BF16)
-        if d > 0:
-            r_b.append(links.start(gx.at[yy, :, pl.ds(6, 6)], ryb.at[d - 1], at_y[d]))
+            both = piece[:, h * 128 : h * 128 + 128].reshape(4, 3, 16, 128) + grecv[row(k), :, part].astype(F32)
+            gown[row(k), :, part] = both
+            gx[row(k), :, part] = both.astype(BF16)
+
+        @pl.when(k < 3)
+        def _():
+            links.at(b_first + k, *along_y(k)).start()
+
+        return carry
+
+    lax.fori_loop(0, 4, give, 0)
+    lax.fori_loop(0, 4, keep, 0)
     r_a = [links.start(gx.at[:, xs[d], pl.ds(0, 6)], rxa.at[d - 1], at_x[d]) for d in range(1, 4)]
 
     arrived(r_b)
@@ -422,6 +458,7 @@
             vmem((8, 5, 192, 128), BF16), vmem((4, 2, 16, 128)), vmem((4, 5, 16, 128), BF16),
             vmem((2, 4, 4, 15, 16, 128), BF16), vmem((4, 4, 16, 128), BF16), vmem((2, 4, 4, 12, 16, 128), BF16),
             vmem((5, 48, 128)), vmem((16, 5, 1, TOK)), vmem((8, 5, 1, TOK)), vmem((4, 5, 1, TOK)),
+            vmem((192, TOK)), vmem((192, TOK)), vmem((TOK, 192), BF16),
             vmem((4, 4, 12, 16, 128), BF16), vmem((4, 4, 12, 16, 128), BF16),
             vmem((4, 4, 12, 16, 128)), vmem((4, 4, 12, 16, 128), BF16),
             vmem((3, 4, 6, 16, 128), BF16), vmem((3, 4, 6, 16, 128), BF16),

time: 99.6 us -> 99.8 us (level)
  no operation moved by 1% of the time
where the time goes in v5:
time: 99.8 us; the launch traced here: 99.3 us
  Pallas kernels  96.2 us (96%)
  local copies, waits for them, and re-layouts  2.43 us (2%)
    pallas_call x1, Pallas kernels, per_device(): pl.pallas_call(body, out_shape=(jax.ShapeDtypeStruct((12, 128), F32), jax...  96.2 us
    unnamed x2, local copies, waits for them, and re-layouts  2.43 us

profile of v5, /device:TPU:1, one launch (start us, length us, event | category | flops | bytes accessed | tf_op | source)
XLA Modules:
  0.0 99.3 jit_solution(15592873168497419992)
XLA Ops:
  0.6 96.2 %shard_map.104 = (f32[12,128]{1,0:T(8,128)}, f32[1,8]{1,0:T(1,128)}) custom-call(bf16[192,1600]{1,0:T(8,128)(2,1)} %act_hbm.1, bf16[160,1600]{1,0:T(8,128)(2,1)} %bitcast.5, bf16[12,160]{1,0:T(8,128)(2,1)} %resid_hbm.1, f32[1,160]{1,0:T(1,128)} %bitcast.6, bf16[12,128]{1,0:T(8,128)(2,1)} %hid_hbm.1, bf16[192,5120]{1,0:T(8,128)(2,1)} %thead_hbm.1, ...), custom_call_target="tpu_custom_call" | custom-call | tf_op jit(solution)/shard_map/pallas_call | solution.py:447
  96.8 1.3 %copy.13 = f32[12,128]{1,0:T(8,128)} copy(f32[12,128]{1,0:T(8,128)} %get-tuple-element.8) | data formatting | bytes 12288
  98.1 1.1 %copy.14 = f32[8]{0:T(128)} copy(f32[8]{0:T(128)} %bitcast.9) | data formatting | bytes 64

commit v6 on v5

--- a/solution.py
+++ b/solution.py
@@ -70,7 +70,7 @@
     act_hbm, down_hbm, resid_hbm, gain_hbm, hid_hbm, thead_hbm, shead_hbm, ids_hbm, counts_hbm,
     grad_out, loss_out,
     act, down, resid, gain, hid, thead, shead, ids, counts,
-    pmain, prem, ppack, psend, precv, rem, rs, gs, u1, u2,
+    pmain, prem, ppack, psend, precv, rem, rs, rp, gs, u1, u2,
     hp, tz, tl, tg, sl, sg, rows48, q1, q2, q3, zs_ref, zt_ref, dl_ref,
     gsend, grecv, gown, gx, rxa, ryb, rya, rxb, sa, sb, fin, fown, fsend, rzl, zsend, rzh,
     load_sem, send_sem, recv_sem,
@@ -143,10 +143,21 @@
 
     loads["resid"].wait()
     loads["gain"].wait()
+    group = iota((16, 128), 1) // 32
     rs[...] = jnp.zeros((16, 256), F32)
     rs[0:12, 0:160] = resid[...].astype(F32)
     gs[...] = jnp.zeros((1, 256), F32)
     gs[:, 0:160] = gain[...]
+    four = gs[:, 128:256]
+    four = four + pltpu.roll(four, 32, 1)
+    four = four + pltpu.roll(four, 64, 1)
+    gains = jnp.where(iota((16, 128), 0) < 12, gs[:, 0:128], four)
+    rp[...] = rs[:, 0:128]
+    for j in range(3):
+        line = rs[4 * j : 4 * j + 1, 128:256]
+        for k in range(1, 4):
+            line = line + pltpu.roll(rs[4 * j + k : 4 * j + k + 1, 128:256], 32 * k, 1)
+        rp[12 + j : 13 + j, :] = line
     rem[...] = jnp.zeros((16, 128), F32)
     zs_ref[...] = jnp.zeros((192, TOK), F32)
     zt_ref[...] = jnp.zeros((192, TOK), F32)
@@ -185,29 +196,6 @@
 
     reorder(0)
 
-    arrived(sums)
-    total = psend[v]
-    for d in range(15):
-        total = total + precv[d]
-    for k in range(4):
-        rows = total[12:15, :] if k == 0 else pltpu.roll(total, 128 - 32 * k, 1)[12:15, :]
-        for j in range(3):
-            rem[4 * j + k : 4 * j + k + 1, 0:32] = rows[j : j + 1, 0:32]
-    pre_a = jnp.where(iota((16, 128), 0) < 12, total, 0.0) + rs[:, 0:128]
-    pre_b = rem[...] + rs[:, 128:256]
-    diagonal = iota((16, 128), 0) == iota((16, 128), 1)
-    column = jnp.sum(pre_a * pre_a + pre_b * pre_b, axis=1, keepdims=True)
-    u1[q] = jnp.sum(jnp.where(diagonal, column, 0.0), axis=0, keepdims=True)
-    squares = [links.start(u1.at[q], u1.at[q], at_q[d]) for d in range(1, 8)]
-
-    gained = pre_b * gs[:, 128:256]
-    moved = gained
-    for h in range(1, 4):
-        moved = jnp.where(zh == h, pltpu.roll(gained, 32 * h, 1), moved)
-    tz[zh, 0] = pre_a * gs[:, 0:128]
-    tz[zh, 1] = moved
-    t_zh = [links.start(tz.at[zh], tz.at[zh], at_zh[d]) for d in range(1, 4)]
-
     def pack(src, dst, tiles):
         for j in range(tiles):
             for k in range(4):
@@ -249,6 +237,24 @@
     pack(sl, sg, 4)
     s_a, s_b = spread(sg, 4)
 
+    arrived(sums)
+    total = psend[v]
+    for d in range(15):
+        total = total + precv[d]
+    pre = total + rp[...]
+    square = pre * pre
+    row_of, lane_of = iota((16, 128), 0), iota((16, 128), 1)
+    diagonal = row_of == lane_of
+    line = jnp.where(diagonal & (row_of < 12), jnp.sum(square, axis=1, keepdims=True), 0.0)
+    for k in range(4):
+        column = jnp.sum(jnp.where(group == k, square, 0.0), axis=1, keepdims=True)
+        line = line + jnp.where((row_of >= 12) & (lane_of == 4 * row_of - 48 + k), column, 0.0)
+    u1[q] = jnp.sum(line, axis=0, keepdims=True)
+    squares = [links.start(u1.at[q], u1.at[q], at_q[d]) for d in range(1, 8)]
+
+    tz[zh] = pre * gains
+    t_zh = [links.start(tz.at[zh], tz.at[zh], at_zh[d]) for d in range(1, 4)]
+
     arrived(squares)
     line = u1[0]
     for k in range(1, 8):
@@ -258,14 +264,23 @@
     s_a, s_b, s_core = spread_on(sg, 4, s_a, s_b)
     reorder(1)
 
+    arrived(t_zh)
+    for k in range(4):
+        side = jnp.zeros((8, 128), F32)
+        for h in range(4):
+            tail = tz[h, 8:16, :]
+            tail = tail if h == k else pltpu.roll(tail, 32 * ((h - k) % 4), 1)
+            side = jnp.where(iota((8, 128), 1) // 32 == h, tail, side)
+        for j in range(3):
+            rem[4 * j + k : 4 * j + k + 1, :] = side[4 + j : 5 + j, :]
+
     arrived(squares)
     line = (u2[0] + u2[1]) + (u2[2] + u2[3])
     column = jnp.sum(jnp.where(diagonal, line, 0.0), axis=1, keepdims=True)
     scale = lax.rsqrt(column / DT + 1e-06)
-    arrived(t_zh)
     for h in range(4):
-        tl[zl, h] = (tz[h, 0] * scale).astype(BF16)
-    tl[zl, 4] = (((tz[0, 1] + tz[1, 1]) + (tz[2, 1] + tz[3, 1])) * scale).astype(BF16)
+        tl[zl, h] = (tz[h] * scale).astype(BF16)
+    tl[zl, 4] = (rem[...] * scale).astype(BF16)
     run = tl.at[zl]
     t_zl = [links.start(run, run, at_zl[d]) for d in range(1, 4)]
     reorder(2)
@@ -306,13 +321,14 @@
         lax.fori_loop(0, 4, one, 0)
 
     def teacher(cc):
-        def one(yy, carry):
-            left = jnp.concatenate([hp[yy * 2 + cc, j] for j in range(5)], axis=1)
-            right = jnp.concatenate([rows_of(tg, cc, yy, j) for j in range(5)], axis=1)
+        def two(half, carry):
+            pairs = [(half * 2 + k, j) for k in range(2) for j in range(5)]
+            left = jnp.concatenate([hp[yy * 2 + cc, j] for yy, j in pairs], axis=1)
+            right = jnp.concatenate([rows_of(tg, cc, yy, j) for yy, j in pairs], axis=1)
             zt_ref[...] += lax.dot_general(left, right, NT, preferred_element_type=F32)
             return carry
 
-        lax.fori_loop(0, 4, one, 0)
+        lax.fori_loop(0, 2, two, 0)
 
     t_a, t_b, t_core = spread_on(tg, 5, t_a, t_b)
     loads["shead"].wait()
@@ -454,8 +470,8 @@
             vmem((12, 128), BF16), vmem((192, DT), BF16), vmem((192, DS), BF16), vmem((1, TOK), jnp.int32), vmem((1, NDOM), jnp.int32),
             vmem((192, 128)), vmem((192, 128)), vmem((48, 128)),
             vmem((16, 16, 128)), vmem((15, 16, 128)), vmem((16, 128)),
-            vmem((16, 256)), vmem((1, 256)), vmem((8, 1, 128)), vmem((4, 1, 128)),
-            vmem((8, 5, 192, 128), BF16), vmem((4, 2, 16, 128)), vmem((4, 5, 16, 128), BF16),
+            vmem((16, 256)), vmem((16, 128)), vmem((1, 256)), vmem((8, 1, 128)), vmem((4, 1, 128)),
+            vmem((8, 5, 192, 128), BF16), vmem((4, 16, 128)), vmem((4, 5, 16, 128), BF16),
             vmem((2, 4, 4, 15, 16, 128), BF16), vmem((4, 4, 16, 128), BF16), vmem((2, 4, 4, 12, 16, 128), BF16),
             vmem((5, 48, 128)), vmem((16, 5, 1, TOK)), vmem((8, 5, 1, TOK)), vmem((4, 5, 1, TOK)),
             vmem((192, TOK)), vmem((192, TOK)), vmem((TOK, 192), BF16),

time: 99.8 us -> 102 us (1.022)
  Pallas kernels: 96.2 us -> 98.7 us
    pallas_call x1, Pallas kernels: 96.2 us -> 98.7 us  [per_device(): pl.pallas_call(body, out_shape=(jax.ShapeDtypeStruct((12, 128), F32), jax...]
where the time goes in v6:
time: 102 us
  Pallas kernels  98.7 us (97%)
  local copies, waits for them, and re-layouts  2.43 us (2%)
    pallas_call x1, Pallas kernels, per_device(): pl.pallas_call(body, out_shape=(jax.ShapeDtypeStruct((12, 128), F32), jax...  98.7 us
    unnamed x2, local copies, waits for them, and re-layouts  2.43 us

profile of v6, /device:TPU:1, one launch (start us, length us, event | category | flops | bytes accessed | tf_op | source)
XLA Modules:
  0.0 101.8 jit_solution(17856300813154680432)
XLA Ops:
  0.6 98.7 %shard_map.104 = (f32[12,128]{1,0:T(8,128)}, f32[1,8]{1,0:T(1,128)}) custom-call(bf16[192,1600]{1,0:T(8,128)(2,1)} %act_hbm.1, bf16[160,1600]{1,0:T(8,128)(2,1)} %bitcast.5, bf16[12,160]{1,0:T(8,128)(2,1)} %resid_hbm.1, f32[1,160]{1,0:T(1,128)} %bitcast.6, bf16[12,128]{1,0:T(8,128)(2,1)} %hid_hbm.1, bf16[192,5120]{1,0:T(8,128)(2,1)} %thead_hbm.1, ...), custom_call_target="tpu_custom_call" | custom-call | tf_op jit(solution)/shard_map/pallas_call | solution.py:463
  99.4 1.3 %copy.13 = f32[12,128]{1,0:T(8,128)} copy(f32[12,128]{1,0:T(8,128)} %get-tuple-element.8) | data formatting | bytes 12288
  100.7 1.1 %copy.14 = f32[8]{0:T(128)} copy(f32[8]{0:T(128)} %bitcast.9) | data formatting | bytes 64

commit v7 on v6

--- a/solution.py
+++ b/solution.py
@@ -233,10 +233,6 @@
             two = buf.at[c, :, xs[4 - d], hi]
             core.append(links.start(two, two, sibling))
 
-    arrived(s_zl)
-    pack(sl, sg, 4)
-    s_a, s_b = spread(sg, 4)
-
     arrived(sums)
     total = psend[v]
     for d in range(15):
@@ -255,13 +251,16 @@
     tz[zh] = pre * gains
     t_zh = [links.start(tz.at[zh], tz.at[zh], at_zh[d]) for d in range(1, 4)]
 
+    arrived(s_zl)
+    pack(sl, sg, 4)
+    s_a, s_b = spread(sg, 4)
+
     arrived(squares)
     line = u1[0]
     for k in range(1, 8):
         line = line + u1[k]
     u2[zh] = line
     squares = [links.start(u2.at[zh], u2.at[zh], at_zh[d]) for d in range(1, 4)]
-    s_a, s_b, s_core = spread_on(sg, 4, s_a, s_b)
     reorder(1)
 
     arrived(t_zh)
@@ -283,6 +282,11 @@
     tl[zl, 4] = (rem[...] * scale).astype(BF16)
     run = tl.at[zl]
     t_zl = [links.start(run, run, at_zl[d]) for d in range(1, 4)]
+    s_a, s_b, s_core = spread_on(sg, 4, s_a, s_b)
+
+    arrived(t_zl)
+    pack(tl, tg, 5)
+    t_a, t_b = spread(tg, 5)
     reorder(2)
 
     loads["ids"].wait()
@@ -300,11 +304,6 @@
         counted = jnp.where(domain == float(k), counts[:, k : k + 1].astype(F32), counted)
     weight = TOK / NDOM / counted
 
-    arrived(t_zl)
-    pack(tl, tg, 5)
-    t_a, t_b = spread(tg, 5)
-    hand_over(sg, 4, s_a, s_b, s_core)
-
     def rows_of(buf, cc, yy, j):
         return buf[cc, yy, :, 3 * j : 3 * j + 3].reshape(TOK, 128)
 
@@ -331,6 +330,7 @@
         lax.fori_loop(0, 2, two, 0)
 
     t_a, t_b, t_core = spread_on(tg, 5, t_a, t_b)
+    hand_over(sg, 4, s_a, s_b, s_core)
     loads["shead"].wait()
     student(c)
     arrived(s_core)

time: 102 us -> 97.8 us (0.959)
  Pallas kernels: 98.7 us -> 94.1 us
    pallas_call x1, Pallas kernels: 98.7 us -> 94.1 us  [per_device(): pl.pallas_call(body, out_shape=(jax.ShapeDtypeStruct((12, 128), F32), jax...]
where the time goes in v7:
time: 97.8 us; the launch traced here: 97.1 us
  Pallas kernels  94.1 us (96%)
  local copies, waits for them, and re-layouts  2.43 us (2%)
    pallas_call x1, Pallas kernels, per_device(): pl.pallas_call(body, out_shape=(jax.ShapeDtypeStruct((12, 128), F32), jax...  94.1 us
    unnamed x2, local copies, waits for them, and re-layouts  2.43 us

profile of v7, /device:TPU:1, one launch (start us, length us, event | category | flops | bytes accessed | tf_op | source)
XLA Modules:
  0.0 97.1 jit_solution(3591791839091447228)
XLA Ops:
  0.6 94.1 %shard_map.104 = (f32[12,128]{1,0:T(8,128)}, f32[1,8]{1,0:T(1,128)}) custom-call(bf16[192,1600]{1,0:T(8,128)(2,1)} %act_hbm.1, bf16[160,1600]{1,0:T(8,128)(2,1)} %bitcast.5, bf16[12,160]{1,0:T(8,128)(2,1)} %resid_hbm.1, f32[1,160]{1,0:T(1,128)} %bitcast.6, bf16[12,128]{1,0:T(8,128)(2,1)} %hid_hbm.1, bf16[192,5120]{1,0:T(8,128)(2,1)} %thead_hbm.1, ...), custom_call_target="tpu_custom_call" | custom-call | tf_op jit(solution)/shard_map/pallas_call | solution.py:463
  94.7 1.3 %copy.13 = f32[12,128]{1,0:T(8,128)} copy(f32[12,128]{1,0:T(8,128)} %get-tuple-element.8) | data formatting | bytes 12288
  96.0 1.1 %copy.14 = f32[8]{0:T(128)} copy(f32[8]{0:T(128)} %bitcast.9) | data formatting | bytes 64

commit v8 on v7

--- a/solution.py
+++ b/solution.py
@@ -120,9 +120,6 @@
     mine[...] = jnp.zeros((16, 128), BF16)
     mine[0:12, :] = hid[...]
 
-    pl.semaphore_wait(barrier, 25)
-    s_zh = [links.start(mine, mine, at_zh[d]) for d in range(1, 4)]
-
     loads["act"].wait()
     loads["down"].wait()
     part = lax.dot_general(act[...], down[...], NT, preferred_element_type=F32)
@@ -139,6 +136,9 @@
         psend[vv, 0:12, :] = pmain[12 * vv : 12 * vv + 12, :]
         psend[vv, 12:15, :] = ppack[3 * vv : 3 * vv + 3, :]
         psend[vv, 15:16, :] = jnp.zeros((1, 128), F32)
+    pl.semaphore_wait(barrier, 25)
+    s_zh = [links.start(mine, mine, at_zh[d]) for d in range(1, 4)]
+
     sums = [links.start(psend.at[vs[d]], precv.at[d - 1], at_v[d]) for d in range(1, 16)]
 
     loads["resid"].wait()

time: 97.8 us -> 97.9 us (level)
  no operation moved by 1% of the time
where the time goes in v8:
time: 97.9 us; the launch traced here: 97.4 us
  Pallas kernels  94.3 us (96%)
  local copies, waits for them, and re-layouts  2.43 us (2%)
    pallas_call x1, Pallas kernels, per_device(): pl.pallas_call(body, out_shape=(jax.ShapeDtypeStruct((12, 128), F32), jax...  94.3 us
    unnamed x2, local copies, waits for them, and re-layouts  2.43 us

profile of v8, /device:TPU:1, one launch (start us, length us, event | category | flops | bytes accessed | tf_op | source)
XLA Modules:
  0.0 97.4 jit_solution(14901059609267244930)
XLA Ops:
  0.6 94.3 %shard_map.104 = (f32[12,128]{1,0:T(8,128)}, f32[1,8]{1,0:T(1,128)}) custom-call(bf16[192,1600]{1,0:T(8,128)(2,1)} %act_hbm.1, bf16[160,1600]{1,0:T(8,128)(2,1)} %bitcast.5, bf16[12,160]{1,0:T(8,128)(2,1)} %resid_hbm.1, f32[1,160]{1,0:T(1,128)} %bitcast.6, bf16[12,128]{1,0:T(8,128)(2,1)} %hid_hbm.1, bf16[192,5120]{1,0:T(8,128)(2,1)} %thead_hbm.1, ...), custom_call_target="tpu_custom_call" | custom-call | tf_op jit(solution)/shard_map/pallas_call | solution.py:463
  94.9 1.3 %copy.13 = f32[12,128]{1,0:T(8,128)} copy(f32[12,128]{1,0:T(8,128)} %get-tuple-element.8) | data formatting | bytes 12288
  96.2 1.1 %copy.14 = f32[8]{0:T(128)} copy(f32[8]{0:T(128)} %bitcast.9) | data formatting | bytes 64
